TPU v7x, 128 devices: a whole 4x4x4 slice. The times are simulated.
128 devices in a mesh: dp: 2 (over z_hi), space: 64 (over y, z_lo, x, core).
Axes of the slice: x: 4, y: 4, z: 4 (z_hi: 2, z_lo: 2; z = z_hi * 2 + z_lo), core: 2. Of those that a mesh axis runs over, the one named last changes fastest.
Arguments:
- features: bfloat16 [2, 64, 128, 256], P('dp', 'space'), may hold values from -50 to 50
- qkv_weight: bfloat16 [256, 768], replicated, may hold values from -0.75 to 0.75
- out_weight: bfloat16 [256, 256], replicated, may hold values from -0.375 to 0.375
- conv_weight: bfloat16 [3, 3, 256, 128], replicated, may hold values from -0.125 to 0.125
- grad_output: bfloat16 [2, 128, 256, 128], P('dp', 'space'), may hold values from -6 to 6
Outputs:
- grad_features: float32 [2, 64, 128, 256], P('dp', 'space')
- grad_qkv: float32 [256, 768], replicated
- grad_out: float32 [256, 256], replicated
- grad_conv: float32 [3, 3, 256, 128], replicated
All inputs are finite; a program needn't handle non-finite values.
Results may differ from a plain program's by a relative error of at most 0.004.
The roundings to bfloat16 on the way count: a program that leaves them out, or rounds other values in their place, can miss the bound.
Values may be sent and summed in bfloat16 or wider, within the bound.
A program may use at most 128 MiB of HBM per device.

v0:
```python
import math

import jax
import jax.numpy as jnp
from jax import lax
from jax.sharding import PartitionSpec as P

HDIM = 64


def extended(cells, sides, width):
    for axis, dim in sides:
        count = lax.axis_size(axis)
        ends = count - 1
        head = lax.slice_in_dim(cells, 0, width, axis=dim)
        tail = lax.slice_in_dim(cells, cells.shape[dim] - width, cells.shape[dim], axis=dim)
        cells = jnp.concatenate(
            [
                lax.ppermute(tail, axis, [(i, (i + 1) % count) for i in range(ends)]),
                cells,
                lax.ppermute(head, axis, [((i + 1) % count, i) for i in range(ends)]),
            ],
            axis=dim,
        )
    return cells


def conv_patches(padded, fine_rows, fine_width, flipped):
    pieces = []
    for row_off in range(3):
        for col_off in range(3):
            row_start = 2 - row_off if flipped else row_off
            col_start = 2 - col_off if flipped else col_off
            pieces.append(
                padded[:, row_start : row_start + fine_rows, col_start : col_start + fine_width, :]
            )
    return jnp.concatenate(pieces, axis=-1)


def shards(features, qkv_weight, out_weight, conv_weight, grad_output):
    samples, row_count, row_width, channels = features.shape
    fine_rows = grad_output.shape[1]
    fine_width = grad_output.shape[2]
    out_channels = grad_output.shape[3]
    head_count = channels // HDIM
    scaling = 1.0 / math.sqrt(HDIM)
    rimmed = extended(grad_output, (("space", 1),), 1)
    rimmed = jnp.pad(rimmed, ((0, 0), (0, 0), (1, 1), (0, 0)))
    flipped_patches = conv_patches(rimmed, fine_rows, fine_width, True)
    kernel = jnp.transpose(conv_weight, (0, 1, 3, 2)).reshape(9 * out_channels, channels)
    grad_up = jnp.einsum(
        "brcy,yx->brcx", flipped_patches, kernel, preferred_element_type=jnp.float32
    )
    grad_hidden = grad_up.reshape(samples, row_count, 2, row_width, 2, channels).sum(axis=(2, 4))
    grad_hidden_low = grad_hidden.astype(jnp.bfloat16)
    grad_attended = jnp.einsum(
        "brcy,xy->brcx", grad_hidden_low, out_weight, preferred_element_type=jnp.float32
    ).astype(jnp.bfloat16)
    gathered = lax.all_gather(features, "space", axis=1, tiled=True)
    seq_len = gathered.shape[1] * row_width
    local_len = row_count * row_width
    block_size = math.gcd(seq_len, 512)
    block_count = seq_len // block_size
    flat_all = gathered.reshape(samples, seq_len, channels)
    flat_local = features.reshape(samples, local_len, channels)
    queries = jnp.einsum(
        "bnx,xy->bny", flat_local, qkv_weight[:, :channels], preferred_element_type=jnp.float32
    ).astype(jnp.bfloat16)
    pair_rows = jnp.einsum(
        "bnx,xy->bny", flat_all, qkv_weight[:, channels:], preferred_element_type=jnp.float32
    ).astype(jnp.bfloat16)
    query_heads = queries.reshape(samples, local_len, head_count, HDIM)
    grad_heads = grad_attended.reshape(samples, local_len, head_count, HDIM)

    def key_block(block_index):
        piece = lax.dynamic_slice_in_dim(pair_rows, block_index * block_size, block_size, 1)
        key_rows = piece[:, :, :channels].reshape(samples, block_size, head_count, HDIM)
        value_rows = piece[:, :, channels:].reshape(samples, block_size, head_count, HDIM)
        scores = (
            jnp.einsum("bqhd,bkhd->bhqk", query_heads, key_rows, preferred_element_type=jnp.float32)
            * scaling
        )
        return (key_rows, value_rows, scores)

    def max_sum(carried, block_index):
        running_max, running_sum = carried
        key_rows, value_rows, scores = key_block(block_index)
        new_max = jnp.maximum(running_max, jnp.max(scores, axis=-1))
        running_sum = running_sum * jnp.exp(running_max - new_max) + jnp.sum(
            jnp.exp(scores - new_max[..., None]), axis=-1
        )
        return ((new_max, running_sum), None)

    stat_shape = (samples, head_count, local_len)
    (running_max, running_sum), unused = lax.scan(
        max_sum,
        (jnp.full(stat_shape, -jnp.inf, jnp.float32), jnp.zeros(stat_shape, jnp.float32)),
        jnp.arange(block_count),
    )
    log_total = running_max + jnp.log(running_sum)

    def forward_block(carried, block_index):
        attended, row_delta = carried
        key_rows, value_rows, scores = key_block(block_index)
        weights = jnp.exp(scores - log_total[..., None])
        attended = attended + jnp.einsum(
            "bhqk,bkhd->bqhd",
            weights.astype(jnp.bfloat16),
            value_rows,
            preferred_element_type=jnp.float32,
        )
        grad_weights = jnp.einsum(
            "bqhd,bkhd->bhqk", grad_heads, value_rows, preferred_element_type=jnp.float32
        )
        row_delta = row_delta + jnp.sum(weights * grad_weights, axis=-1)
        return ((attended, row_delta), None)

    head_shape = (samples, local_len, head_count, HDIM)
    (attended, row_delta), unused = lax.scan(
        forward_block,
        (jnp.zeros(head_shape, jnp.float32), jnp.zeros(stat_shape, jnp.float32)),
        jnp.arange(block_count),
    )

    def backward_block(carried, block_index):
        grad_queries, partial_rows = carried
        key_rows, value_rows, scores = key_block(block_index)
        weights = jnp.exp(scores - log_total[..., None])
        grad_weights = jnp.einsum(
            "bqhd,bkhd->bhqk", grad_heads, value_rows, preferred_element_type=jnp.float32
        )
        grad_scores = (weights * (grad_weights - row_delta[..., None])).astype(jnp.bfloat16)
        grad_queries = grad_queries + jnp.einsum(
            "bhqk,bkhd->bqhd", grad_scores, key_rows, preferred_element_type=jnp.float32
        )
        grad_keys = (
            jnp.einsum(
                "bhqk,bqhd->bkhd", grad_scores, query_heads, preferred_element_type=jnp.float32
            )
            * scaling
        )
        grad_values = jnp.einsum(
            "bhqk,bqhd->bkhd",
            weights.astype(jnp.bfloat16),
            grad_heads,
            preferred_element_type=jnp.float32,
        )
        both_grads = jnp.concatenate(
            [
                grad_keys.reshape(samples, block_size, channels),
                grad_values.reshape(samples, block_size, channels),
            ],
            axis=-1,
        )
        partial_rows = lax.dynamic_update_slice_in_dim(
            partial_rows, both_grads, block_index * block_size, 1
        )
        return ((grad_queries, partial_rows), None)

    (grad_queries, partial_rows), unused = lax.scan(
        backward_block,
        (
            jnp.zeros(head_shape, jnp.float32),
            jnp.zeros((samples, seq_len, 2 * channels), jnp.float32),
        ),
        jnp.arange(block_count),
    )
    grad_pairs = lax.psum_scatter(partial_rows, "space", scatter_dimension=1, tiled=True)
    grad_queries = (grad_queries * scaling).reshape(samples, local_len, channels)
    grad_proj = jnp.concatenate([grad_queries, grad_pairs], axis=-1).astype(jnp.bfloat16)
    attended_low = attended.reshape(samples, local_len, channels).astype(jnp.bfloat16)
    grad_features = grad_hidden + jnp.einsum(
        "bny,xy->bnx", grad_proj, qkv_weight, preferred_element_type=jnp.float32
    ).reshape(samples, row_count, row_width, channels)
    term_qkv = jnp.einsum("bnx,bny->xy", flat_local, grad_proj, preferred_element_type=jnp.float32)
    term_out = jnp.einsum(
        "bnx,bny->xy",
        attended_low,
        grad_hidden_low.reshape(samples, local_len, channels),
        preferred_element_type=jnp.float32,
    )
    hidden = (
        features.astype(jnp.float32)
        + jnp.einsum(
            "bnx,xy->bny", attended_low, out_weight, preferred_element_type=jnp.float32
        ).reshape(samples, row_count, row_width, channels)
    ).astype(jnp.bfloat16)
    rim_hidden = extended(hidden, (("space", 1),), 1)
    upsampled = jnp.repeat(jnp.repeat(rim_hidden, 2, axis=1), 2, axis=2)[:, 1:-1]
    upsampled = jnp.pad(upsampled, ((0, 0), (0, 0), (1, 1), (0, 0)))
    patches = conv_patches(upsampled, fine_rows, fine_width, False)
    term_conv = jnp.einsum(
        "brcx,brcy->xy", patches, grad_output, preferred_element_type=jnp.float32
    ).reshape(3, 3, channels, out_channels)
    sum_qkv, sum_out, sum_conv = lax.psum((term_qkv, term_out, term_conv), ("dp", "space"))
    total_samples = samples * lax.axis_size("dp")
    coarse_scale = 1.0 / math.sqrt(total_samples * seq_len)
    fine_scale = 1.0 / math.sqrt(total_samples * fine_rows * lax.axis_size("space") * fine_width)
    return (grad_features, coarse_scale * sum_qkv, coarse_scale * sum_out, fine_scale * sum_conv)


def solution(mesh):
    in_specs = (P("dp", "space", None, None), P(), P(), P(), P("dp", "space", None, None))
    out_specs = (P("dp", "space", None, None), P(), P(), P())
    return jax.shard_map(shards, mesh=mesh, in_specs=in_specs, out_specs=out_specs, check_vma=False)
```

profile of v0, /device:TPU:1, one launch (start us, length us, event | category | flops | bytes accessed | tf_op | source)
XLA Modules:
  0.0 800.1 jit_solution(11987727110098570028)
XLA Ops:
  8.9 3.3 collective-permute-start.1
  12.2 3.1 collective-permute-start
  15.3 1.1 convolution_convert_fusion.2
  16.5 1.3 copy.42
  19.3 1.2 copy.41
  21.4 97.9 %all-gather.2.cloned.1.call-done = bf16[1,64,128,256]{3,2,0,1:T(8,128)(2,1)} async-done(((bf16[1,1,128,256]{3,2,0,1:T(8,128)(2,1)}), bf16[1,64,128,256]{3,2,0,1:T(8,128)(2,1)}) %all-gather.2.cloned.1.call-update) | async-done | bytes 4194320 | tf_op jit(solution)/shard_map/all_gather | solution.py:59
  119.3 7.8 fusion.20
  127.0 11.8 %copy.49 = bf16[1,8192,512]{1,2,0:T(8,128)(2,1)} copy(bf16[1,8192,512]{2,1,0:T(8,128)(2,1)} %fusion.20) | data formatting | bytes 16777216
  138.9 45.1 %while.39 = (s32[]{:T(128)}, f32[1,4,128]{2,1,0:T(4,128)S(1)}, f32[1,4,128]{2,1,0:T(4,128)S(1)}, s32[16]{0:T(128)S(1)}, bf16[1,8192,512]{1,2,0:T(8,128)(2,1)}, /...) while((s32[]{:T(128)}, f32[1,4,128]{2,1,0:T(4,128)S(1)}, ...), condition=%wide.region_4.5_spmd.clone, body=%wide.region_1.4_spmd.clone.sunk | while | flops 34605572 | bytes 2975926 | solution.py:95
  183.9 53.4 %while.40 = (s32[]{:T(128)}, f32[1,128,4,64]{1,3,2,0:T(8,128)S(1)}, f32[1,4,128]{2,1,0:T(4,128)S(1)}, s32[16]{0:T(128)S(1)}, bf16[1,8192,512]{1,2,0:T(8,128)(2,1...) while((s32[]{:T(128)}, f32[1,128,4,64]{1,3,2,0:T(8,128)S(1)}, ...), condition=%wide.region_7.8_spmd.clone, body=%wide.region_5.7_spmd.clone.sunk | while | flops 102040072 | bytes 5384414 | solution.py:119
  185.2 1.1 constant_dynamic-slice_fusion.9
  188.5 1.1 constant_dynamic-slice_fusion.9
  191.9 1.1 constant_dynamic-slice_fusion.9
  195.2 1.1 constant_dynamic-slice_fusion.9
  198.5 1.1 constant_dynamic-slice_fusion.9
  201.9 1.1 constant_dynamic-slice_fusion.9
  205.2 1.1 constant_dynamic-slice_fusion.9
  208.5 1.1 constant_dynamic-slice_fusion.9
  211.9 1.1 constant_dynamic-slice_fusion.9
  215.2 1.1 constant_dynamic-slice_fusion.9
  218.5 1.1 constant_dynamic-slice_fusion.9
  221.9 1.1 constant_dynamic-slice_fusion.9
  225.2 1.1 constant_dynamic-slice_fusion.9
  228.6 1.1 constant_dynamic-slice_fusion.9
  231.9 1.1 constant_dynamic-slice_fusion.9
  235.2 1.1 constant_dynamic-slice_fusion.9
  237.3 7.8 broadcast_in_dim.20
  245.1 79.3 %while.41 = (s32[]{:T(128)}, f32[1,128,4,64]{1,3,2,0:T(8,128)S(1)}, f32[1,8192,512]{1,2,0:T(8,128)}, s32[16]{0:T(128)S(1)}, bf16[1,8192,512]{1,2,0:T(8,128)(2,1)...) while((s32[]{:T(128)}, f32[1,128,4,64]{1,3,2,0:T(8,128)S(1)}, ...), condition=%wide.region_9.10_spmd.clone, body=%wide.region_8.9_spmd.clone.sunk | while | flops 169803776 | bytes 10227945 | solution.py:160
  246.3 1.1 constant_dynamic-slice_fusion.10
  249.0 1.1 maximum_dynamic-update-slice_fusion.2
  251.3 1.1 constant_dynamic-slice_fusion.10
  254.0 1.1 maximum_dynamic-update-slice_fusion.2
  256.3 1.1 constant_dynamic-slice_fusion.10
  258.9 1.1 maximum_dynamic-update-slice_fusion.2
  261.2 1.1 constant_dynamic-slice_fusion.10
  263.9 1.1 maximum_dynamic-update-slice_fusion.2
  266.2 1.1 constant_dynamic-slice_fusion.10
  268.9 1.1 maximum_dynamic-update-slice_fusion.2
  271.2 1.1 constant_dynamic-slice_fusion.10
  273.8 1.1 maximum_dynamic-update-slice_fusion.2
  276.1 1.1 constant_dynamic-slice_fusion.10
  281.1 1.1 constant_dynamic-slice_fusion.10
  286.0 1.1 constant_dynamic-slice_fusion.10
  288.7 1.1 maximum_dynamic-update-slice_fusion.2
  291.0 1.1 constant_dynamic-slice_fusion.10
  293.6 1.1 maximum_dynamic-update-slice_fusion.2
  296.0 1.1 constant_dynamic-slice_fusion.10
  300.9 1.1 constant_dynamic-slice_fusion.10
  305.9 1.1 constant_dynamic-slice_fusion.10
  308.5 1.1 maximum_dynamic-update-slice_fusion.2
  310.8 1.1 constant_dynamic-slice_fusion.10
  315.8 1.1 constant_dynamic-slice_fusion.10
  320.7 1.1 constant_dynamic-slice_fusion.10
  325.4 2.2 collective-permute-start.3
  327.6 3.6 collective-permute-start.2
  334.1 1.4 copy-done.2
  335.5 2.8 copy.50
  339.1 1.1 copy.61
  340.2 288.0 %reduce-scatter.2.cloned.1.call-done = f32[1,128,512]{1,2,0:T(8,128)} async-done(((f32[1,8192,512]{1,2,0:T(8,128)}), f32[1,128,512]{1,2,0:T(8,128)}) %reduce-scatter.2.cloned.1.call-update) | async-done | bytes 262160 | tf_op jit(solution)/shard_map/reduce_scatter | solution.py:168
  629.2 1.1 convolution_bitcast_fusion.2
  631.3 158.0 %all-reduce.5.cloned.1.call-done = (f32[256,768]{0,1:T(8,128)}, f32[256,256]{1,0:T(8,128)}, f32[3,3,256,128]{3,2,1,0:T(8,128)}) async-done(((f32[256,768]{0,1:T(8,128)}, f32[256,256]{1,0:T(8,128)}, f32[3,3,256,128]{3,2,1,0:T(8,128)}), (f32[256,768]{0,1:T(8,128)}, f32[256,256]{1,0:T(8,128)}, f32[3,3,256,128]{3,2,1,0:T(8,128)})) %all-reduce.5.cloned.1.call-update) | async-done | bytes 2228240 | tf_op jit(solution)/shard_map/psum | solution.py:195
  789.3 1.3 broadcast_multiply_fusion.1
  790.6 1.1 copy.51
  792.5 1.1 broadcast_multiply_fusion
  (368 shorter events, 111.5 us)
Async XLA Ops:
  7.2 13.9 %copy-start = (bf16[256,256]{1,0:T(8,128)(2,1)S(1)}, bf16[256,256]{1,0:T(8,128)(2,1)}, u32[]{:S(2)}) copy-start(bf16[256,256]{1,0:T(8,128)(2,1)} %param.13) | copy-start | bytes 393220
  7.2 11.8 %copy-start.1 = (bf16[1,2,256,128]{3,2,1,0:T(8,128)(2,1)S(1)}, bf16[1,2,256,128]{3,2,1,0:T(8,128)(2,1)}, u32[]{:S(2)}) copy-start(bf16[1,2,256,128]{3,2,1,0:T(8,128)(2,1)} %param.15) | copy-start | bytes 393220
  7.2 112.1 %all-gather.2.cloned.1.call-start = ((), (), s32[]{:S(2)}) async-start(), calls=%async_computation.1 | async-start | bytes 4259840 | tf_op jit(solution)/shard_map/all_gather | solution.py:59
  7.9 620.3 %reduce-scatter.2.cloned.1.call-start = ((), (), s32[]{:S(2)}) async-start(), calls=%async_computation.2 | async-start | bytes 17039360 | tf_op jit(solution)/shard_map/reduce_scatter | solution.py:168
  8.9 9.0 %collective-permute-start.1 = (bf16[1,1,256,128]{3,2,1,0:T(8,128)(2,1)S(1)}, bf16[1,1,256,128]{3,2,1,0:T(8,128)(2,1)S(1)}, u32[]{:S(2)}, u32[]{:S(2)}) collective-permute-start(bf16[1,1,256,128]{3,2,1,0:T(8,128)(2,1)S(1)} %get-tuple-element.376), channel_id=1, source_target_pairs={{1,0},{2,1},{3,2},{4,3},{5,4},{6,5},{7,6},{8,7},{9,8},{10,9},{11,1... | collective-permute-start | bytes 196616 | tf_op jit(solution)/shard_map/ppermute | solution.py:21
  12.2 5.7 collective-permute-start
  19.3 99.9 %copy-start.3 = (bf16[256,768]{1,0:T(8,128)(2,1)S(1)}, bf16[256,768]{1,0:T(8,128)(2,1)}, u32[]{:S(2)}) copy-start(bf16[256,768]{1,0:T(8,128)(2,1)} %param.12) | copy-start | bytes 1179652
  324.4 0.8 copy-start.5
  324.4 464.8 %all-reduce.5.cloned.1.call-start = ((), (), s32[]{:S(2)}) async-start(), calls=%async_computation.3 | async-start | bytes 4456448 | tf_op jit(solution)/shard_map/psum | solution.py:195
  325.4 7.3 collective-permute-start.3
  327.6 5.1 collective-permute-start.2
  334.1 1.4 copy-start.2
  338.3 290.8 %copy-start.6 = (bf16[1,1,128,256]{3,2,1,0:T(8,128)(2,1)S(1)}, bf16[1,1,128,256]{3,2,1,0:T(8,128)(2,1)}, u32[]{:S(2)}) copy-start(bf16[1,1,128,256]{3,2,1,0:T(8,128)(2,1)} %param.11) | copy-start | bytes 196612
  338.3 290.8 %copy-start.7 = (bf16[1,128,4,64]{1,3,2,0:T(8,128)(2,1)S(1)}, bf16[1,128,4,64]{1,3,2,0:T(8,128)(2,1)}, u32[]{:S(2)}) copy-start(bf16[1,128,4,64]{1,3,2,0:T(8,128)(2,1)} %multiply_convert_fusion) | copy-start | bytes 196612
  789.3 2.5 copy-start.8
  789.3 3.2 copy-start.4
Sparse Core Ops, SparseCore 0:
  9.7 109.4 all-gather.1
  324.6 303.6 reduce-scatter.1
  634.1 155.1 all-reduce.4
where the time goes:
time: 802 us; the launch traced here: 800 us
  waiting for transfers between devices  545 us (68%)
  local copies, waits for them, and re-layouts  110 us (14%)
  matrix products  59.6 us (7%)
  loops' own time  33.5 us (4%)
  other arithmetic  25.9 us (3%)
  between operations  14.2 us (2%)
  starting transfers between devices  12.3 us (2%)
    reduce_scatter x1, waiting for transfers between devices, shards(): lax.psum_scatter(partial_rows, 'space', scatter_dimension=1, tiled=True)  288 us
    psum x1, waiting for transfers between devices, shards(): lax.psum((term_qkv, term_out, term_conv), ('dp', 'space'))  158 us
    all_gather x1, waiting for transfers between devices, shards(): gathered = lax.all_gather(features, 'space', axis=1, tiled=True)  97.9 us
    slice x32, local copies, waits for them, and re-layouts, key_block(): piece[:, :, :channels].reshape(samples, block_size, head_count, HDIM)  32.7 us
    dynamic_slice x48, local copies, waits for them, and re-layouts, shards(): lax.scan(max_sum, (jnp.full(stat_shape, -jnp.inf, jnp.float32), jnp.zeros...  28.1 us
    dot_general x48, matrix products, key_block(): jnp.einsum('bqhd,bkhd->bhqk', query_heads, key_rows, preferred_element_ty...  17.5 us
    slice x16, local copies, waits for them, and re-layouts, key_block(): piece[:, :, channels:].reshape(samples, block_size, head_count, HDIM)  17.2 us
    unnamed x35, local copies, waits for them, and re-layouts  17.1 us
  transfers between devices with their start and end apart: 7, of which 3 were waited for; matrix products, arithmetic and copies ran while one was open for 2% of the time, Pallas kernels for 0%

commit v1 on v0

v1 whole, which is shorter than its diff:
```python
import math

import jax
import jax.numpy as jnp
from jax import lax
from jax.experimental import pallas as pl
from jax.experimental.pallas import tpu as pltpu
from jax.sharding import PartitionSpec as P

MESH = pl.DeviceIdType.MESH
F32 = jnp.float32
BF16 = jnp.bfloat16
HDIM = 64
HEADS = 4
CH = 256
CO = 128
ROW = 128
RING = 4
CHUNK = RING * ROW
CHUNKS = 8
STACK = 2 * HEADS * ROW
HALF = STACK // 2
SUB = 32
REST_ROWS = 3072
QKV_ROWS = 1536
AG_MSGS = 41
ST_MSGS = 13
RS_MSGS = 17


def nt(a, b):
    return lax.dot_general(a, b, (((1,), (1,)), ((), ())), preferred_element_type=F32)


def tn(a, b):
    return lax.dot_general(a, b, (((0,), (0,)), ((), ())), preferred_element_type=F32)


def nn(a, b):
    return jnp.dot(a, b, preferred_element_type=F32)


class Message:
    def __init__(self, src, dst, landing, sems, slot, device):
        send, recv = sems
        self.out = pltpu.make_async_remote_copy(
            src_ref=src, dst_ref=dst, send_sem=send.at[slot], recv_sem=recv.at[slot], device_id=device, device_id_type=MESH
        )
        self.into = pltpu.make_async_remote_copy(
            src_ref=landing, dst_ref=landing, send_sem=send.at[slot], recv_sem=recv.at[slot], device_id=device, device_id_type=MESH
        )

    def start(self):
        self.out.start()

    def arrived(self):
        self.into.wait_recv()

    def sent(self):
        self.out.wait_send()


class Place:
    def __init__(self):
        self.d = lax.axis_index("dp")
        self.s = lax.axis_index("space")
        s = self.s
        self.c = lax.rem(s, 2)
        self.x = lax.rem(s // 2, RING)
        self.zl = lax.rem(s // 8, 2)
        self.y = s // 16
        self.zo = 1 - self.zl

    def at(self, d=None, y=None, z=None, x=None, c=None):
        d = self.d if d is None else d
        y = self.y if y is None else y
        z = self.zl if z is None else z
        x = self.x if x is None else x
        c = self.c if c is None else c
        return (d, ((y * 2 + z) * RING + x) * 2 + c)

    def line(self, step):
        return (self.d, lax.rem(self.s + step + 64, 64))

    def ring_x(self, step):
        return self.at(x=lax.rem(self.x + step + RING, RING))

    def ring_y(self, step):
        return self.at(y=lax.rem(self.y + step + RING, RING))

    def first(self, t, step):
        hit = t == 0
        return self.at(
            x=jnp.where(hit, lax.rem(self.x + step + RING, RING), self.x),
            y=jnp.where(hit, self.y, lax.rem(self.y + step + RING, RING)),
        )

    def second(self, t, step):
        return self.first(1 - t, step)

    def coords(self, t):
        return jnp.where(t == 0, self.y, self.x), jnp.where(t == 0, self.x, self.y)


class Gather:
    def __init__(self, place, buf, sems, base):
        self.place, self.buf, self.sems, self.count, self.base = place, buf, sems, 0, base
        half = ROW // 2
        low, high = pl.ds(0, half), pl.ds(half, half)
        s0, f0 = place.coords(place.zl)
        s1, f1 = place.coords(place.zo)
        m = {"z": self.make((place.zl, s0, f0), (place.zo, s1, f1), place.at(z=place.zo))}
        for r in (0, 1):
            t = place.zl if r == 0 else place.zo
            s, f = (s0, f0) if r == 0 else (s1, f1)
            sm, sp, s2 = (lax.rem(s + k, RING) for k in (3, 1, 2))
            fm, fp, f2 = (lax.rem(f + k, RING) for k in (3, 1, 2))
            up, down = place.first(t, 1), place.first(t, -1)
            m[r, "1+"] = self.make((t, s, f), (t, s, fm), up)
            m[r, "1-"] = self.make((t, s, f), (t, s, fp), down)
            m[r, "1f+"] = self.make((t, s, fm, low), (t, s, f2, low), up)
            m[r, "1f-"] = self.make((t, s, fp, high), (t, s, f2, high), down)
            up, down = place.second(t, 1), place.second(t, -1)
            for q, g in enumerate((f, fm, fp, f2)):
                m[r, q, "2+"] = self.make((t, s, g), (t, sm, g), up)
                m[r, q, "2-"] = self.make((t, s, g), (t, sp, g), down)
                m[r, q, "2f+"] = self.make((t, sm, g, low), (t, s2, g, low), up)
                m[r, q, "2f-"] = self.make((t, sp, g, high), (t, s2, g, high), down)
        self.m = m

    def make(self, src, landing, device):
        slot = self.base + self.count
        self.count += 1
        src = self.buf.at[src]
        return Message(src, src, self.buf.at[landing], self.sems, slot, device)

    def go(self, *keys):
        for key in keys:
            self.m[key].start()

    def begin(self):
        self.go("z", (0, "1+"), (0, "1-"), (0, 0, "2+"), (0, 0, "2-"))

    def other(self):
        self.m["z"].arrived()
        self.go((1, "1+"), (1, "1-"), (1, 0, "2+"), (1, 0, "2-"))

    def near(self, r):
        self.m[r, "1+"].arrived()
        self.go((r, "1f+"), (r, 1, "2+"), (r, 1, "2-"))
        self.m[r, "1-"].arrived()
        self.go((r, "1f-"), (r, 2, "2+"), (r, 2, "2-"))

    def pass_on(self, r, *blocks):
        for q in blocks:
            self.m[r, q, "2+"].arrived()
            self.go((r, q, "2f+"))
            self.m[r, q, "2-"].arrived()
            self.go((r, q, "2f-"))

    def far(self, r):
        self.m[r, "1f+"].arrived()
        self.m[r, "1f-"].arrived()
        self.go((r, 3, "2+"), (r, 3, "2-"))

    def last(self, r):
        for q in range(4):
            self.m[r, q, "2f+"].arrived()
            self.m[r, q, "2f-"].arrived()

    def finish(self):
        for message in self.m.values():
            message.sent()


class StatGather:
    def __init__(self, place, buf, sems, base):
        s0, f0 = place.coords(place.zl)
        s1, f1 = place.coords(place.zo)
        src = buf.at[place.zl, s0, f0]
        self.z = Message(src, src, buf.at[place.zo, s1, f1], sems, base, place.at(z=place.zo))
        self.one, self.two = {}, {}
        slot = base + 1
        for r in (0, 1):
            t = place.zl if r == 0 else place.zo
            s, f = (s0, f0) if r == 0 else (s1, f1)
            for k in (1, 3, 2):
                src = buf.at[t, s, f]
                self.one[r, k] = Message(src, src, buf.at[t, s, lax.rem(f + RING - k, RING)], sems, slot, place.first(t, k))
                src = buf.at[t, s]
                self.two[r, k] = Message(src, src, buf.at[t, lax.rem(s + RING - k, RING)], sems, slot + 1, place.second(t, k))
                slot += 2

    def begin(self):
        self.z.start()
        for k in (1, 3, 2):
            self.one[0, k].start()

    def other(self):
        self.z.arrived()
        for k in (1, 3, 2):
            self.one[1, k].start()

    def spread(self, r):
        for k in (1, 3, 2):
            self.one[r, k].arrived()
        for k in (1, 3, 2):
            self.two[r, k].start()

    def last(self):
        for message in self.two.values():
            message.arrived()

    def finish(self):
        for message in (self.z, *self.one.values(), *self.two.values()):
            message.sent()


class Total:
    def __init__(self, place, rows, part, half_out, half_in, mid, mid_out, mid_in, low, low_out, low_in, zed, done, sems, base):
        self.place, self.rows, self.part = place, rows, part
        self.half_out, self.half_in, self.mid, self.mid_out, self.mid_in = half_out, half_in, mid, mid_out, mid_in
        self.low, self.low_out, self.low_in, self.zed, self.done = low, low_out, low_in, zed, done
        n2, n8, n32 = rows // 2, rows // 8, rows // 32
        self.n2, self.n8, self.n32 = n2, n8, n32
        c = place.c
        t = c
        v, u = place.coords(t)
        self.u, self.v = u, v
        self.z = place.d * 2 + place.zl
        sib = place.at(c=1 - c)
        slot = base
        self.core = Message(half_out, half_out_dst(half_in), half_in, sems, slot, sib)
        slot += 1
        self.by_u, self.by_v, self.by_z, self.back_v, self.back_u = {}, {}, {}, {}, {}
        for i, k in enumerate((1, 3, 2)):
            self.by_u[k] = Message(mid_out.at[i], mid_in.at[i], mid_in.at[i], sems, slot, place.first(t, k))
            self.by_v[k] = Message(low_out.at[i], low_in.at[i], low_in.at[i], sems, slot + 1, place.second(t, k))
            zt = lax.rem(self.z + k, 4)
            zs = lax.rem(self.z + 4 - k, 4)
            self.by_z[k] = Message(
                zed.at[self.z], zed.at[self.z], zed.at[zs], sems, slot + 2, place.at(d=zt // 2, z=lax.rem(zt, 2))
            )
            mine = done.at[self.span(c, u, v)]
            self.back_v[k] = Message(
                mine, mine, done.at[self.span(c, u, lax.rem(v + 4 - k, 4))], sems, slot + 3, place.second(t, k)
            )
            mine = done.at[self.span(c, u)]
            self.back_u[k] = Message(
                mine, mine, done.at[self.span(c, lax.rem(u + 4 - k, 4))], sems, slot + 4, place.first(t, k)
            )
            slot += 5
        mine = done.at[self.span(c)]
        self.back_c = Message(mine, mine, done.at[self.span(1 - c)], sems, slot, sib)

    def span(self, c, u=None, v=None):
        if u is None:
            return pl.ds(pl.multiple_of(c * self.n2, 16), self.n2)
        if v is None:
            return pl.ds(pl.multiple_of(c * self.n2 + u * self.n8, 16), self.n8)
        return pl.ds(pl.multiple_of(c * self.n2 + u * self.n8 + v * self.n32, 16), self.n32)

    def begin(self):
        self.half_out[...] = self.part[self.span(1 - self.place.c)].astype(BF16)
        self.core.start()

    def step_u(self):
        self.core.arrived()
        self.mid[...] = self.part[self.span(self.place.c)] + self.half_in[...].astype(F32)
        for i, k in enumerate((1, 3, 2)):
            start = pl.multiple_of(lax.rem(self.u + k, 4) * self.n8, 16)
            self.mid_out[i] = self.mid[pl.ds(start, self.n8)].astype(BF16)
            self.by_u[k].start()

    def step_v(self):
        for k in (1, 3, 2):
            self.by_u[k].arrived()
        start = pl.multiple_of(self.u * self.n8, 16)
        self.low[...] = self.mid[pl.ds(start, self.n8)] + (
            (self.mid_in[0].astype(F32) + self.mid_in[1].astype(F32)) + self.mid_in[2].astype(F32)
        )
        for i, k in enumerate((1, 3, 2)):
            start = pl.multiple_of(lax.rem(self.v + k, 4) * self.n32, 16)
            self.low_out[i] = self.low[pl.ds(start, self.n32)].astype(BF16)
            self.by_v[k].start()

    def step_z(self):
        for k in (1, 3, 2):
            self.by_v[k].arrived()
        start = pl.multiple_of(self.v * self.n32, 16)
        total = self.low[pl.ds(start, self.n32)] + (
            (self.low_in[0].astype(F32) + self.low_in[1].astype(F32)) + self.low_in[2].astype(F32)
        )
        self.zed[self.z] = total.astype(BF16)
        for k in (1, 3, 2):
            self.by_z[k].start()

    def return_v(self):
        for k in (1, 3, 2):
            self.by_z[k].arrived()
        total = (self.zed[0].astype(F32) + self.zed[1].astype(F32)) + (self.zed[2].astype(F32) + self.zed[3].astype(F32))
        self.done[self.span(self.place.c, self.u, self.v)] = total.astype(BF16)
        for k in (1, 3, 2):
            self.back_v[k].start()

    def return_u(self):
        for k in (1, 3, 2):
            self.back_v[k].arrived()
        for k in (1, 3, 2):
            self.back_u[k].start()

    def return_c(self):
        for k in (1, 3, 2):
            self.back_u[k].arrived()
        self.back_c.start()

    def last(self):
        self.back_c.arrived()

    def finish(self):
        self.core.sent()
        for group in (self.by_u, self.by_v, self.by_z, self.back_v, self.back_u):
            for message in group.values():
                message.sent()
        self.back_c.sent()


def half_out_dst(half_in):
    return half_in


def total_scratch(rows):
    return [
        pltpu.VMEM((rows, 128), F32),
        pltpu.VMEM((rows // 2, 128), BF16),
        pltpu.VMEM((rows // 2, 128), BF16),
        pltpu.VMEM((rows // 2, 128), F32),
        pltpu.VMEM((3, rows // 8, 128), BF16),
        pltpu.VMEM((3, rows // 8, 128), BF16),
        pltpu.VMEM((rows // 8, 128), F32),
        pltpu.VMEM((3, rows // 32, 128), BF16),
        pltpu.VMEM((3, rows // 32, 128), BF16),
        pltpu.VMEM((4, rows // 32, 128), BF16),
        pltpu.VMEM((rows, 128), BF16),
    ]


def head_mask(shape, h):
    lane = lax.broadcasted_iota(jnp.int32, shape, len(shape) - 1)
    return jnp.logical_and(lane >= h * HDIM, lane < (h + 1) * HDIM)


def stack_heads(ref, half, rows):
    for h in range(HEADS):
        start = (half * HEADS + h) * ROW
        ref[start : start + ROW] = jnp.where(head_mask(rows.shape, h), rows, jnp.zeros_like(rows))


def unstack_heads(ref, half):
    out = jnp.zeros((ROW, CH), F32)
    for h in range(HEADS):
        start = (half * HEADS + h) * ROW
        out = jnp.where(head_mask((ROW, CH), h), ref[start : start + ROW], out)
    return out


def moved(rows, step):
    n = rows.shape[0]
    index = lax.broadcasted_iota(jnp.int32, rows.shape, 0)
    if step == 1:
        return jnp.where(index == n - 1, 0.0, pltpu.roll(rows, n - 1, 0))
    return jnp.where(index == 0, 0.0, pltpu.roll(rows, 1, 0))


def kernel(
    feat, wqkv, wout, wconv, go,
    gf, gqkv, gout, gconv,
    feats, grads, stats, sib_feat, sib_grad, fine, rim,
    keys, values, qm, dm,
    scores, gweights, low_w, low_g, acc_a, acc_b,
    run_m, run_l, run_d, tri_out, tri_in,
    part_out, part_in, pair_out, pair_in, ghid, glow, gproj, hid,
    *rest,
):
    rest_total, qkv_total, (send, recv) = rest[:11], rest[11:22], rest[22:]
    sems = (send, recv)
    place = Place()
    c, s, zl = place.c, place.s, place.zl
    sib = place.at(c=1 - c)
    above, below = place.line(-1), place.line(1)

    base = 0
    fg = Gather(place, feats, sems, base)
    base += AG_MSGS
    dg = Gather(place, grads, sems, base)
    base += AG_MSGS
    sg = StatGather(place, stats, sems, base)
    base += ST_MSGS
    rest_sum = Total(place, REST_ROWS, *rest_total, sems, base)
    base += RS_MSGS
    qkv_sum = Total(place, QKV_ROWS, *qkv_total, sems, base)
    base += RS_MSGS
    sib_f = Message(feat, sib_feat, sib_feat, sems, base, sib)
    down_fine = Message(fine.at[2], fine.at[0], fine.at[0], sems, base + 1, below)
    up_fine = Message(fine.at[1], fine.at[3], fine.at[3], sems, base + 2, above)
    s0, f0 = place.coords(zl)
    own = (zl, s0, f0)
    sib_g = Message(grads.at[own], sib_grad, sib_grad, sems, base + 3, sib)
    tri = Message(tri_out, tri_in, tri_in, sems, base + 4, sib)
    parts = Message(part_out, part_in, part_in, sems, base + 5, sib)
    down_hid = Message(hid, rim.at[0], rim.at[0], sems, base + 6, below)
    up_hid = Message(hid, rim.at[1], rim.at[1], sems, base + 7, above)
    pairs = Message(pair_out, pair_in, pair_in, sems, base + 8, sib)

    barrier = pltpu.get_barrier_semaphore()
    peers = [sib, place.at(z=place.zo), above, below]
    peers += [place.ring_x(k) for k in (1, 2, 3)] + [place.ring_y(k) for k in (1, 2, 3)]
    peers += [place.at(d=1 - place.d), place.at(d=1 - place.d, z=place.zo)]
    for peer in peers:
        pl.semaphore_signal(barrier, inc=1, device_id=peer, device_id_type=MESH)
    pl.semaphore_wait(barrier, len(peers))

    feats[own] = feat[...]
    fine[1] = go[0]
    fine[2] = go[1]
    down_fine.start()
    up_fine.start()
    fg.begin()
    sib_f.start()

    down_fine.arrived()
    up_fine.arrived()
    rows = fine[...]
    top = jnp.where(s > 0, rows[0], jnp.zeros_like(rows[0]))
    bottom = jnp.where(s < 63, rows[3], jnp.zeros_like(rows[3]))
    lines = [top, rows[1], rows[2], bottom]
    main = jnp.zeros((2 * ROW, CH), F32)
    plus = jnp.zeros((2 * ROW, CH), F32)
    minus = jnp.zeros((2 * ROW, CH), F32)
    for a in range(3):
        both = jnp.concatenate([lines[2 - a], lines[3 - a]], axis=0)
        w0, w1, w2 = wconv[3 * a], wconv[3 * a + 1], wconv[3 * a + 2]
        main = main + nt(both, jnp.concatenate([w1, w0], axis=1)) + nt(both, jnp.concatenate([w2, w1], axis=1))
        plus = plus + nt(both[:, :CO], w0)
        minus = minus + nt(both[:, CO:], w2)
    main, plus, minus = (m[:ROW] + m[ROW:] for m in (main, plus, minus))
    hidden_grad = main + moved(plus, 1) + moved(minus, -1)
    ghid[...] = hidden_grad
    hidden_low = hidden_grad.astype(BF16)
    glow[...] = hidden_low
    own_grad = nt(hidden_low, wout[...]).astype(BF16)
    grads[own] = own_grad
    sib_g.start()
    fg.other()
    fg.near(0)
    fg.pass_on(0, 0)
    dg.begin()

    def scaled_queries(rows):
        whole = nn(rows, wqkv[:, :CH]).astype(BF16)
        return (whole.astype(F32) * (1.0 / math.sqrt(HDIM))).astype(BF16)

    def stack_keys(rows, half):
        whole = nn(rows, wqkv[:, CH:]).astype(BF16)
        stack_heads(qm, half, whole[:, :CH])
        stack_heads(dm, half, whole[:, CH:])

    stack_heads(qm, 0, scaled_queries(feat[...]))
    stack_heads(dm, 0, own_grad)
    fg.near(1)
    fg.pass_on(1, 0)
    sib_f.arrived()
    stack_heads(qm, 1, scaled_queries(sib_feat[...]))
    sib_g.arrived()
    stack_heads(dm, 1, sib_grad[...])

    run_m[...] = jnp.full((STACK, 128), -1e30, F32)
    run_l[...] = jnp.zeros((STACK, 128), F32)
    run_d[...] = jnp.zeros((STACK, 128), F32)

    def where_is(j):
        role, order = lax.rem(j, 2), j // 2
        t = jnp.where(role == 0, zl, place.zo)
        offset = jnp.where(order == 0, 0, jnp.where(order == 1, 3, jnp.where(order == 2, 1, 2)))
        second, _ = place.coords(t)
        return t, lax.rem(second + offset, RING)

    def at_step(j, steps):
        for when, act in steps.items():
            pl.when(j == when)(act)

    def stat_steps():
        def first(j, unused):
            def act0():
                fg.far(0)

            def act1():
                fg.far(1)

            def act2():
                fg.pass_on(0, 1, 2, 3)
                dg.other()

            def act3():
                fg.pass_on(1, 1, 2, 3)
                dg.near(0)
                dg.pass_on(0, 0)

            def act4():
                dg.near(1)
                dg.pass_on(1, 0)

            def act6():
                fg.last(0)
                dg.far(0)

            def act7():
                fg.last(1)
                dg.far(1)

            at_step(j, {0: act0, 1: act1, 2: act2, 3: act3, 4: act4, 6: act6, 7: act7})
            t, second = where_is(j)
            block = feats[t, second].reshape(CHUNK, CH)
            whole = nn(block, wqkv[:, CH:]).astype(BF16)
            keys[j] = whole[:, :CH]
            values[j] = whole[:, CH:]
            scores[j] = nt(qm[...], keys[j])
            gweights[j] = nt(dm[...], values[j])

            def tile(i, unused):
                span = pl.ds(pl.multiple_of(i * SUB, SUB), SUB)
                cut = [pl.ds(b * 128, 128) for b in range(RING)]
                sc = [scores[j, span, k] for k in cut]
                old = run_m[span]
                new = jnp.maximum(jnp.maximum(jnp.maximum(sc[0], sc[1]), jnp.maximum(sc[2], sc[3])), old)
                shrink = jnp.exp(old - new)
                total, dot = run_l[span] * shrink, run_d[span] * shrink
                for k in range(RING):
                    w = jnp.exp(sc[k] - new)
                    total = total + w
                    dot = dot + w * gweights[j, span, cut[k]]
                run_m[span] = new
                run_l[span] = total
                run_d[span] = dot
                return unused

            lax.fori_loop(0, STACK // SUB, tile, 0, unroll=4)
            return unused

        lax.fori_loop(0, CHUNKS, first, 0)

    stat_steps()

    lane = lax.broadcasted_iota(jnp.int32, (ROW, 128), 1)
    mine = [jnp.zeros((ROW, 128), F32), jnp.ones((ROW, 128), F32), jnp.zeros((ROW, 128), F32)]
    theirs = list(mine)
    for half in (0, 1):
        for h in range(HEADS):
            g = half * HEADS + h
            span = slice(g * ROW, (g + 1) * ROW)
            m = run_m[span]
            top = jnp.max(m, axis=1, keepdims=True)
            e = jnp.exp(m - top)
            cols = [
                top,
                jnp.sum(run_l[span] * e, axis=1, keepdims=True),
                jnp.sum(run_d[span] * e, axis=1, keepdims=True),
            ]
            for k in range(3):
                mine[k] = jnp.where(lane == g, cols[k], mine[k])
                theirs[k] = jnp.where(lane == (1 - half) * HEADS + h, cols[k], theirs[k])
    for k in range(3):
        tri_out[k] = theirs[k]
    tri.start()
    tri.arrived()
    top = jnp.maximum(mine[0], tri_in[0])
    ea, eb = jnp.exp(mine[0] - top), jnp.exp(tri_in[0] - top)
    total = mine[1] * ea + tri_in[1] * eb
    delta = (mine[2] * ea + tri_in[2] * eb) / total
    lse = top + jnp.log(total)
    stats[own] = jnp.concatenate([jnp.transpose(lse)[:HEADS], jnp.transpose(delta)[:HEADS]], axis=0)
    sg.begin()
    for g in range(2 * HEADS):
        span = slice(g * ROW, (g + 1) * ROW)
        run_m[span] = jnp.broadcast_to(lse[:, g : g + 1], (ROW, 128))
        run_l[span] = jnp.broadcast_to(delta[:, g : g + 1], (ROW, 128))

    acc_a[...] = jnp.zeros((STACK, CH), F32)
    acc_b[...] = jnp.zeros((STACK, CH), F32)

    def forward(j, unused):
        def act0():
            sg.other()
            dg.pass_on(0, 1, 2)

        def act1():
            dg.pass_on(1, 1, 2)
            sg.spread(0)

        def act2():
            dg.pass_on(0, 3)
            sg.spread(1)

        def act3():
            dg.pass_on(1, 3)

        at_step(j, {0: act0, 1: act1, 2: act2, 3: act3})

        for half in (0, 1):

            def tile(i, unused, half=half):
                own_span = pl.ds(pl.multiple_of(i * SUB, SUB), SUB)
                span = pl.ds(pl.multiple_of(half * HALF + i * SUB, SUB), SUB)
                lse_t, delta_t = run_m[span], run_l[span]
                for b in range(RING):
                    cut = pl.ds(b * 128, 128)
                    w = jnp.exp(scores[j, span, cut] - lse_t)
                    low_w[own_span, cut] = w.astype(BF16)
                    low_g[own_span, cut] = (w * (gweights[j, span, cut] - delta_t)).astype(BF16)
                return unused

            lax.fori_loop(0, HALF // SUB, tile, 0, unroll=4)
            into = slice(half * HALF, (half + 1) * HALF)
            acc_a[into] += nn(low_w[...], values[j])
            acc_b[into] += nn(low_g[...], keys[j])
        return unused

    lax.fori_loop(0, CHUNKS, forward, 0)
    part_out[0] = unstack_heads(acc_a, 1)
    part_out[1] = unstack_heads(acc_b, 1)
    parts.start()
    attended_mine = unstack_heads(acc_a, 0)
    gq_mine = unstack_heads(acc_b, 0)
    parts.arrived()
    attended = (attended_mine + part_in[0]).astype(BF16)
    gproj[:, :CH] = ((gq_mine + part_in[1]) * (1.0 / math.sqrt(HDIM))).astype(BF16)
    hid[...] = (feat[...].astype(F32) + nn(attended, wout[...])).astype(BF16)
    down_hid.start()
    up_hid.start()
    out_part = tn(attended, glow[...])
    rest_sum.part[2304:2560] = out_part[:, :128]
    rest_sum.part[2560:2816] = out_part[:, 128:]
    rest_sum.part[2816:] = jnp.zeros((REST_ROWS - 2816, 128), F32)

    down_hid.arrived()
    up_hid.arrived()
    mid = hid[...]
    over = jnp.where(s > 0, rim[0], jnp.zeros_like(mid))
    under = jnp.where(s < 63, rim[1], jnp.zeros_like(mid))
    sides = []
    for r in (0, 1):
        wide = go[r].astype(F32)
        even, odd = wide[:, :CO], wide[:, CO:]
        sides.append(jnp.concatenate([even, odd, moved(even, 1), moved(odd, -1)], axis=1).astype(BF16))
    products = {
        (0, 0): tn(mid, sides[0]),
        (0, 1): tn(mid, sides[1]),
        (-1, 0): tn(over, sides[0]),
        (1, 1): tn(under, sides[1]),
    }
    for a, whole in enumerate(
        (
            products[-1, 0] + products[0, 1],
            products[0, 0] + products[0, 1],
            products[0, 0] + products[1, 1],
        )
    ):
        even, odd, even1, odd1 = (whole[:, k * CO : (k + 1) * CO] for k in range(4))
        rest_sum.part[(3 * a) * CH : (3 * a + 1) * CH] = even1 + odd
        rest_sum.part[(3 * a + 1) * CH : (3 * a + 2) * CH] = even + odd
        rest_sum.part[(3 * a + 2) * CH : (3 * a + 3) * CH] = even + odd1
    rest_sum.begin()

    stack_keys(feat[...], 0)
    stack_keys(sib_feat[...], 1)
    dg.last(0)
    dg.last(1)
    sg.last()
    acc_a[...] = jnp.zeros((STACK, CH), F32)
    acc_b[...] = jnp.zeros((STACK, CH), F32)

    def backward(j, unused):
        at_step(
            j,
            {
                1: rest_sum.step_u,
                2: rest_sum.step_v,
                3: rest_sum.step_z,
                4: rest_sum.return_v,
                5: rest_sum.return_u,
                6: rest_sum.return_c,
            },
        )
        t, second = where_is(j)
        block = grads[t, second].reshape(CHUNK, CH)
        asked = scaled_queries(feats[t, second].reshape(CHUNK, CH))
        scores[0] = nt(qm[...], asked)
        gweights[0] = nt(dm[...], block)
        for half in (0, 1):
            for h in range(HEADS):

                def tile(i, unused, h=h, half=half):
                    own_span = pl.ds(pl.multiple_of(h * ROW + i * SUB, SUB), SUB)
                    span = pl.ds(pl.multiple_of((half * HEADS + h) * ROW + i * SUB, SUB), SUB)
                    for b in range(RING):
                        cut = pl.ds(b * 128, 128)
                        w = jnp.exp(scores[0, span, cut] - stats[t, second, b, h : h + 1, :])
                        low_w[own_span, cut] = w.astype(BF16)
                        low_g[own_span, cut] = (
                            w * (gweights[0, span, cut] - stats[t, second, b, HEADS + h : HEADS + h + 1, :])
                        ).astype(BF16)
                    return unused

                lax.fori_loop(0, ROW // SUB, tile, 0, unroll=4)
            into = slice(half * HALF, (half + 1) * HALF)
            acc_a[into] += nn(low_g[...], asked)
            acc_b[into] += nn(low_w[...], block)
        return unused

    lax.fori_loop(0, CHUNKS, backward, 0)
    pair_out[:, :CH] = unstack_heads(acc_a, 1)
    pair_out[:, CH:] = unstack_heads(acc_b, 1)
    pairs.start()
    gk_mine = unstack_heads(acc_a, 0)
    gv_mine = unstack_heads(acc_b, 0)
    pairs.arrived()
    gproj[:, CH : 2 * CH] = (gk_mine + pair_in[:, :CH]).astype(BF16)
    gproj[:, 2 * CH :] = (gv_mine + pair_in[:, CH:]).astype(BF16)
    proj = gproj[...]
    qkv_part = tn(feat[...], proj)
    for k in range(6):
        qkv_sum.part[k * CH : (k + 1) * CH] = qkv_part[:, k * 128 : (k + 1) * 128]
    qkv_sum.begin()
    gf[...] = ghid[...] + nt(proj, wqkv[...])
    coarse = 1.0 / math.sqrt(2 * 64 * ROW)
    fine_scale = 1.0 / math.sqrt(2 * 128 * 256)
    qkv_sum.step_u()
    rest_sum.last()
    gconv[...] = rest_sum.done[:2304].astype(F32) * fine_scale
    gout[:, :128] = rest_sum.done[2304:2560].astype(F32) * coarse
    gout[:, 128:] = rest_sum.done[2560:2816].astype(F32) * coarse
    qkv_sum.step_v()
    qkv_sum.step_z()
    qkv_sum.return_v()
    qkv_sum.return_u()
    qkv_sum.return_c()
    qkv_sum.last()
    for k in range(6):
        gqkv[:, k * 128 : (k + 1) * 128] = qkv_sum.done[k * CH : (k + 1) * CH].astype(F32) * coarse

    for group in (fg, dg, sg, rest_sum, qkv_sum):
        group.finish()
    for message in (sib_f, down_fine, up_fine, sib_g, tri, parts, down_hid, up_hid, pairs):
        message.sent()


def shards(features, qkv_weight, out_weight, conv_weight, grad_output):
    messages = 2 * AG_MSGS + ST_MSGS + 2 * RS_MSGS + 9
    whole = pl.BlockSpec(memory_space=pltpu.VMEM)
    gf, gqkv, gout, gconv = pl.pallas_call(
        kernel,
        out_shape=[
            jax.ShapeDtypeStruct((ROW, CH), F32),
            jax.ShapeDtypeStruct((CH, 3 * CH), F32),
            jax.ShapeDtypeStruct((CH, CH), F32),
            jax.ShapeDtypeStruct((9 * CH, CO), F32),
        ],
        in_specs=[whole] * 5,
        out_specs=[whole] * 4,
        scratch_shapes=[
            pltpu.VMEM((2, RING, RING, ROW, CH), BF16),
            pltpu.VMEM((2, RING, RING, ROW, CH), BF16),
            pltpu.VMEM((2, RING, RING, 2 * HEADS, ROW), F32),
            pltpu.VMEM((ROW, CH), BF16),
            pltpu.VMEM((ROW, CH), BF16),
            pltpu.VMEM((4, ROW, 2 * CO), BF16),
            pltpu.VMEM((2, ROW, CH), BF16),
            pltpu.VMEM((CHUNKS, CHUNK, CH), BF16),
            pltpu.VMEM((CHUNKS, CHUNK, CH), BF16),
            pltpu.VMEM((STACK, CH), BF16),
            pltpu.VMEM((STACK, CH), BF16),
            pltpu.VMEM((CHUNKS, STACK, CHUNK), F32),
            pltpu.VMEM((CHUNKS, STACK, CHUNK), F32),
            pltpu.VMEM((HALF, CHUNK), BF16),
            pltpu.VMEM((HALF, CHUNK), BF16),
            pltpu.VMEM((STACK, CH), F32),
            pltpu.VMEM((STACK, CH), F32),
            pltpu.VMEM((STACK, 128), F32),
            pltpu.VMEM((STACK, 128), F32),
            pltpu.VMEM((STACK, 128), F32),
            pltpu.VMEM((3, ROW, 128), F32),
            pltpu.VMEM((3, ROW, 128), F32),
            pltpu.VMEM((2, ROW, CH), F32),
            pltpu.VMEM((2, ROW, CH), F32),
            pltpu.VMEM((ROW, 2 * CH), F32),
            pltpu.VMEM((ROW, 2 * CH), F32),
            pltpu.VMEM((ROW, CH), F32),
            pltpu.VMEM((ROW, CH), BF16),
            pltpu.VMEM((ROW, 3 * CH), BF16),
            pltpu.VMEM((ROW, CH), BF16),
            *total_scratch(REST_ROWS),
            *total_scratch(QKV_ROWS),
            pltpu.SemaphoreType.DMA((messages,)),
            pltpu.SemaphoreType.DMA((messages,)),
        ],
        compiler_params=pltpu.CompilerParams(
            collective_id=0, has_side_effects=True, vmem_limit_bytes=63 * 1024 * 1024
        ),
    )(
        features.reshape(ROW, CH),
        qkv_weight,
        out_weight,
        conv_weight.reshape(9, CH, CO),
        grad_output.reshape(2, ROW, 2 * CO),
    )
    return (
        gf.reshape(1, 1, ROW, CH),
        gqkv,
        gout,
        gconv.reshape(3, 3, CH, CO),
    )


def solution(mesh):
    in_specs = (P("dp", "space", None, None), P(), P(), P(), P("dp", "space", None, None))
    out_specs = (P("dp", "space", None, None), P(), P(), P())
    return jax.shard_map(shards, mesh=mesh, in_specs=in_specs, out_specs=out_specs, check_vma=False)
```

time: 802 us -> 127 us (0.16)
  waiting for transfers between devices: 545 us -> 0 us
  Pallas kernels: 0 us -> 119 us
  local copies, waits for them, and re-layouts: 110 us -> 7.07 us
  matrix products: 59.6 us -> 0 us
  loops' own time: 33.5 us -> 0 us
  other arithmetic: 25.9 us -> 0 us
  between operations: 14.2 us -> 0.66 us
  starting transfers between devices: 12.3 us -> 0 us
    reduce_scatter x1 -> x0, waiting for transfers between devices: 288 us -> none  [shards(): lax.psum_scatter(partial_rows, 'space', scatter_dimension=1, tiled=True)]
    psum x1 -> x0, waiting for transfers between devices: 158 us -> none  [shards(): lax.psum((term_qkv, term_out, term_conv), ('dp', 'space'))]
    pallas_call x0 -> x1, Pallas kernels: none -> 119 us  [shards(): pl.pallas_call(kernel, out_shape=[jax.ShapeDtypeStruct((ROW, CH), F32), j...]
    all_gather x1 -> x0, waiting for transfers between devices: 97.9 us -> none  [shards(): gathered = lax.all_gather(features, 'space', axis=1, tiled=True)]
    dot_general x153 -> x0, matrix products: 59.6 us -> none  [the longest x48 17.5 us: key_block(): jnp.einsum('bqhd,bkhd->bhqk', query_heads, key_rows, preferred_element_ty...]
    slice x50 -> x0, local copies, waits for them, and re-layouts: 50.8 us -> none  [the longest x32 32.7 us: key_block(): piece[:, :, :channels].reshape(samples, block_size, head_count, HDIM)]
    another operation x3 -> x0, loops' own time: 33.5 us -> none  [the longest x1 11.2 us: shards(): lax.scan(max_sum, (jnp.full(stat_shape, -jnp.inf, jnp.float32), jnp.zeros...]
    dynamic_slice x48 -> x0, local copies, waits for them, and re-layouts: 28.1 us -> none  [shards(): lax.scan(max_sum, (jnp.full(stat_shape, -jnp.inf, jnp.float32), jnp.zeros...]
  transfers between devices with their start and end apart: 7 -> 0, of which waited for: 3 -> 0; matrix products, arithmetic and copies ran while one was open for 2% -> 0% of each run, Pallas kernels for 0% -> 0%
where the time goes in v1:
time: 127 us
  Pallas kernels  119 us (94%)
  local copies, waits for them, and re-layouts  7.07 us (6%)
    pallas_call x1, Pallas kernels, shards(): pl.pallas_call(kernel, out_shape=[jax.ShapeDtypeStruct((ROW, CH), F32), j...  119 us
    unnamed x8, local copies, waits for them, and re-layouts  5.46 us

profile of v1, /device:TPU:1, one launch (start us, length us, event | category | flops | bytes accessed | tf_op | source)
XLA Modules:
  0.0 127.1 jit_solution(17507708370913396541)
XLA Ops:
  0.6 1.6 %reshape.25.go = bf16[2,128,256]{2,1,0:T(8,128)(2,1)} reshape(bf16[1,2,256,128]{3,2,1,0:T(8,128)(2,1)} %param.9) | data formatting | bytes 262144 | tf_op jit(solution)/shard_map/reshape | solution.py:814
  2.2 119.4 %shard_map.84 = (f32[128,256]{1,0:T(8,128)}, f32[256,768]{1,0:T(8,128)}, f32[256,256]{1,0:T(8,128)}, f32[2304,128]{1,0:T(8,128)}) custom-call(bf16[128,256]{1,0:T(8,128)(2,1)} %bitcast.9, bf16[256,768]{1,0:T(8,128)(2,1)} %wqkv.1, bf16[256,256]{1,0:T(8,128)(2,1)} %wout.1, bf16[9,256,128]{2,1,0:T(8,128)(2,1)} %bitcast.7, bf16[2,128,256]{2,1,0:T(8,128)(2,1)} %reshape.25.go), custom_call_target="tpu_custom_call" | custom-call | tf_op jit(solution)/shard_map/pallas_call | solution.py:760
  121.6 0.0 copy-start.1
  121.6 0.0 copy-start
  121.6 1.7 %copy.13 = f32[1,1,128,256]{3,2,1,0:T(8,128)} copy(f32[1,1,128,256]{3,2,1,0:T(8,128)} %bitcast.8) | data formatting | bytes 262144
  123.3 2.1 %copy.14 = f32[256,768]{1,0:T(8,128)} copy(f32[256,768]{1,0:T(8,128)} %get-tuple-element.17) | data formatting | bytes 1572864
  125.4 0.0 copy-done.1
  125.4 0.7 copy.15
  126.1 0.0 copy-done
  126.1 1.0 copy.16
Async XLA Ops:
  121.6 3.8 %copy-start.1 = (f32[256,256]{1,0:T(8,128)S(1)}, f32[256,256]{1,0:T(8,128)}, u32[]{:S(2)}) copy-start(f32[256,256]{1,0:T(8,128)} %get-tuple-element.18) | copy-start | bytes 786436
  121.6 4.5 %copy-start = (f32[2304,128]{1,0:T(8,128)S(1)}, f32[2304,128]{1,0:T(8,128)}, u32[]{:S(2)}) copy-start(f32[2304,128]{1,0:T(8,128)} %get-tuple-element.11) | copy-start | bytes 3538948

commit v2 on v1

--- a/solution.py
+++ b/solution.py
@@ -21,11 +21,12 @@
 STACK = 2 * HEADS * ROW
 HALF = STACK // 2
 SUB = 32
-REST_ROWS = 3072
-QKV_ROWS = 1536
+REST_ROWS = 3584
+QKV_ROWS = 1024
+PLANE = [(k % 4, k // 4) for k in range(1, 16)]
 AG_MSGS = 41
-ST_MSGS = 13
-RS_MSGS = 17
+ST_MSGS = 31
+RS_MSGS = 35
 
 
 def nt(a, b):
@@ -88,6 +89,13 @@
     def ring_y(self, step):
         return self.at(y=lax.rem(self.y + step + RING, RING))
 
+    def plane(self, dx, dy, z=None):
+        return self.at(x=lax.rem(self.x + dx + RING, RING), y=lax.rem(self.y + dy + RING, RING), z=z)
+
+    def back(self, t, dx, dy):
+        x, y = lax.rem(self.x + RING - dx, RING), lax.rem(self.y + RING - dy, RING)
+        return t, jnp.where(t == 0, y, x), jnp.where(t == 0, x, y)
+
     def first(self, t, step):
         hit = t == 0
         return self.at(
@@ -103,8 +111,9 @@
 
 
 class Gather:
-    def __init__(self, place, buf, sems, base):
+    def __init__(self, place, buf, sems, base, direct):
         self.place, self.buf, self.sems, self.count, self.base = place, buf, sems, 0, base
+        self.direct = direct
         half = ROW // 2
         low, high = pl.ds(0, half), pl.ds(half, half)
         s0, f0 = place.coords(place.zl)
@@ -118,8 +127,11 @@
             up, down = place.first(t, 1), place.first(t, -1)
             m[r, "1+"] = self.make((t, s, f), (t, s, fm), up)
             m[r, "1-"] = self.make((t, s, f), (t, s, fp), down)
-            m[r, "1f+"] = self.make((t, s, fm, low), (t, s, f2, low), up)
-            m[r, "1f-"] = self.make((t, s, fp, high), (t, s, f2, high), down)
+            if direct:
+                m[r, "12"] = self.make((t, s, f), (t, s, f2), place.first(t, 2))
+            else:
+                m[r, "1f+"] = self.make((t, s, fm, low), (t, s, f2, low), up)
+                m[r, "1f-"] = self.make((t, s, fp, high), (t, s, f2, high), down)
             up, down = place.second(t, 1), place.second(t, -1)
             for q, g in enumerate((f, fm, fp, f2)):
                 m[r, q, "2+"] = self.make((t, s, g), (t, sm, g), up)
@@ -138,18 +150,22 @@
         for key in keys:
             self.m[key].start()
 
+    def ring(self, r):
+        self.go((r, "1+"), (r, "1-"), *([(r, "12")] if self.direct else []), (r, 0, "2+"), (r, 0, "2-"))
+
     def begin(self):
-        self.go("z", (0, "1+"), (0, "1-"), (0, 0, "2+"), (0, 0, "2-"))
+        self.go("z")
+        self.ring(0)
 
     def other(self):
         self.m["z"].arrived()
-        self.go((1, "1+"), (1, "1-"), (1, 0, "2+"), (1, 0, "2-"))
+        self.ring(1)
 
     def near(self, r):
         self.m[r, "1+"].arrived()
-        self.go((r, "1f+"), (r, 1, "2+"), (r, 1, "2-"))
+        self.go(*([] if self.direct else [(r, "1f+")]), (r, 1, "2+"), (r, 1, "2-"))
         self.m[r, "1-"].arrived()
-        self.go((r, "1f-"), (r, 2, "2+"), (r, 2, "2-"))
+        self.go(*([] if self.direct else [(r, "1f-")]), (r, 2, "2+"), (r, 2, "2-"))
 
     def pass_on(self, r, *blocks):
         for q in blocks:
@@ -159,8 +175,11 @@
             self.go((r, q, "2f-"))
 
     def far(self, r):
-        self.m[r, "1f+"].arrived()
-        self.m[r, "1f-"].arrived()
+        if self.direct:
+            self.m[r, "12"].arrived()
+        else:
+            self.m[r, "1f+"].arrived()
+            self.m[r, "1f-"].arrived()
         self.go((r, 3, "2+"), (r, 3, "2-"))
 
     def last(self, r):
@@ -179,169 +198,119 @@
         s1, f1 = place.coords(place.zo)
         src = buf.at[place.zl, s0, f0]
         self.z = Message(src, src, buf.at[place.zo, s1, f1], sems, base, place.at(z=place.zo))
-        self.one, self.two = {}, {}
+        self.wide = ([], [])
         slot = base + 1
         for r in (0, 1):
             t = place.zl if r == 0 else place.zo
-            s, f = (s0, f0) if r == 0 else (s1, f1)
-            for k in (1, 3, 2):
-                src = buf.at[t, s, f]
-                self.one[r, k] = Message(src, src, buf.at[t, s, lax.rem(f + RING - k, RING)], sems, slot, place.first(t, k))
-                src = buf.at[t, s]
-                self.two[r, k] = Message(src, src, buf.at[t, lax.rem(s + RING - k, RING)], sems, slot + 1, place.second(t, k))
-                slot += 2
+            src = buf.at[place.back(t, 0, 0)]
+            for dx, dy in PLANE:
+                self.wide[r].append(Message(src, src, buf.at[place.back(t, dx, dy)], sems, slot, place.plane(dx, dy)))
+                slot += 1
 
     def begin(self):
         self.z.start()
-        for k in (1, 3, 2):
-            self.one[0, k].start()
+        for message in self.wide[0]:
+            message.start()
 
     def other(self):
         self.z.arrived()
-        for k in (1, 3, 2):
-            self.one[1, k].start()
-
-    def spread(self, r):
-        for k in (1, 3, 2):
-            self.one[r, k].arrived()
-        for k in (1, 3, 2):
-            self.two[r, k].start()
+        for message in self.wide[1]:
+            message.start()
 
     def last(self):
-        for message in self.two.values():
+        for message in (*self.wide[0], *self.wide[1]):
             message.arrived()
 
     def finish(self):
-        for message in (self.z, *self.one.values(), *self.two.values()):
+        for message in (self.z, *self.wide[0], *self.wide[1]):
             message.sent()
 
 
 class Total:
-    def __init__(self, place, rows, part, half_out, half_in, mid, mid_out, mid_in, low, low_out, low_in, zed, done, sems, base):
-        self.place, self.rows, self.part = place, rows, part
-        self.half_out, self.half_in, self.mid, self.mid_out, self.mid_in = half_out, half_in, mid, mid_out, mid_in
-        self.low, self.low_out, self.low_in, self.zed, self.done = low, low_out, low_in, zed, done
-        n2, n8, n32 = rows // 2, rows // 8, rows // 32
-        self.n2, self.n8, self.n32 = n2, n8, n32
+    def __init__(self, place, rows, part, half_in, mid_out, mid_in, zed, done, sems, base):
+        self.place, self.part, self.half_in = place, part, half_in
+        self.mid_out, self.mid_in, self.zed, self.done = mid_out, mid_in, zed, done
+        self.half, self.piece = rows // 2, rows // 32
         c = place.c
-        t = c
-        v, u = place.coords(t)
-        self.u, self.v = u, v
+        self.mine = place.y * RING + place.x
         self.z = place.d * 2 + place.zl
         sib = place.at(c=1 - c)
-        slot = base
-        self.core = Message(half_out, half_out_dst(half_in), half_in, sems, slot, sib)
-        slot += 1
-        self.by_u, self.by_v, self.by_z, self.back_v, self.back_u = {}, {}, {}, {}, {}
-        for i, k in enumerate((1, 3, 2)):
-            self.by_u[k] = Message(mid_out.at[i], mid_in.at[i], mid_in.at[i], sems, slot, place.first(t, k))
-            self.by_v[k] = Message(low_out.at[i], low_in.at[i], low_in.at[i], sems, slot + 1, place.second(t, k))
-            zt = lax.rem(self.z + k, 4)
-            zs = lax.rem(self.z + 4 - k, 4)
-            self.by_z[k] = Message(
-                zed.at[self.z], zed.at[self.z], zed.at[zs], sems, slot + 2, place.at(d=zt // 2, z=lax.rem(zt, 2))
+        away = part.at[self.span(1 - c)]
+        self.core = Message(away, half_in, half_in, sems, base, sib)
+        slot = base + 1
+        self.out, self.by_z, self.back = [], [], []
+        here = done.at[self.span(c, self.mine)]
+        for k, (dx, dy) in enumerate(PLANE):
+            x, y = lax.rem(place.x + dx, RING), lax.rem(place.y + dy, RING)
+            src = mid_out.at[pl.ds(pl.multiple_of((y * RING + x) * self.piece, 16), self.piece)]
+            self.out.append(Message(src, mid_in.at[k], mid_in.at[k], sems, slot, place.plane(dx, dy)))
+            x, y = lax.rem(place.x + RING - dx, RING), lax.rem(place.y + RING - dy, RING)
+            self.back.append(
+                Message(here, here, done.at[self.span(c, y * RING + x)], sems, slot + 1, place.plane(dx, dy))
             )
-            mine = done.at[self.span(c, u, v)]
-            self.back_v[k] = Message(
-                mine, mine, done.at[self.span(c, u, lax.rem(v + 4 - k, 4))], sems, slot + 3, place.second(t, k)
-            )
-            mine = done.at[self.span(c, u)]
-            self.back_u[k] = Message(
-                mine, mine, done.at[self.span(c, lax.rem(u + 4 - k, 4))], sems, slot + 4, place.first(t, k)
-            )
-            slot += 5
-        mine = done.at[self.span(c)]
-        self.back_c = Message(mine, mine, done.at[self.span(1 - c)], sems, slot, sib)
-
-    def span(self, c, u=None, v=None):
-        if u is None:
-            return pl.ds(pl.multiple_of(c * self.n2, 16), self.n2)
-        if v is None:
-            return pl.ds(pl.multiple_of(c * self.n2 + u * self.n8, 16), self.n8)
-        return pl.ds(pl.multiple_of(c * self.n2 + u * self.n8 + v * self.n32, 16), self.n32)
+            slot += 2
+        for k in (1, 3, 2):
+            to, of = lax.rem(self.z + k, 4), lax.rem(self.z + 4 - k, 4)
+            src = zed.at[self.z]
+            self.by_z.append(Message(src, src, zed.at[of], sems, slot, place.at(d=to // 2, z=lax.rem(to, 2))))
+            slot += 1
+        src = done.at[self.span(c)]
+        self.across = Message(src, src, done.at[self.span(1 - c)], sems, slot, sib)
+
+    def span(self, c, piece=None):
+        if piece is None:
+            return pl.ds(pl.multiple_of(c * self.half, 16), self.half)
+        return pl.ds(pl.multiple_of(c * self.half + piece * self.piece, 16), self.piece)
 
     def begin(self):
-        self.half_out[...] = self.part[self.span(1 - self.place.c)].astype(BF16)
         self.core.start()
 
-    def step_u(self):
+    def scatter(self):
         self.core.arrived()
-        self.mid[...] = self.part[self.span(self.place.c)] + self.half_in[...].astype(F32)
-        for i, k in enumerate((1, 3, 2)):
-            start = pl.multiple_of(lax.rem(self.u + k, 4) * self.n8, 16)
-            self.mid_out[i] = self.mid[pl.ds(start, self.n8)].astype(BF16)
-            self.by_u[k].start()
-
-    def step_v(self):
-        for k in (1, 3, 2):
-            self.by_u[k].arrived()
-        start = pl.multiple_of(self.u * self.n8, 16)
-        self.low[...] = self.mid[pl.ds(start, self.n8)] + (
-            (self.mid_in[0].astype(F32) + self.mid_in[1].astype(F32)) + self.mid_in[2].astype(F32)
-        )
-        for i, k in enumerate((1, 3, 2)):
-            start = pl.multiple_of(lax.rem(self.v + k, 4) * self.n32, 16)
-            self.low_out[i] = self.low[pl.ds(start, self.n32)].astype(BF16)
-            self.by_v[k].start()
-
-    def step_z(self):
-        for k in (1, 3, 2):
-            self.by_v[k].arrived()
-        start = pl.multiple_of(self.v * self.n32, 16)
-        total = self.low[pl.ds(start, self.n32)] + (
-            (self.low_in[0].astype(F32) + self.low_in[1].astype(F32)) + self.low_in[2].astype(F32)
-        )
-        self.zed[self.z] = total.astype(BF16)
-        for k in (1, 3, 2):
-            self.by_z[k].start()
-
-    def return_v(self):
-        for k in (1, 3, 2):
-            self.by_z[k].arrived()
-        total = (self.zed[0].astype(F32) + self.zed[1].astype(F32)) + (self.zed[2].astype(F32) + self.zed[3].astype(F32))
-        self.done[self.span(self.place.c, self.u, self.v)] = total.astype(BF16)
-        for k in (1, 3, 2):
-            self.back_v[k].start()
-
-    def return_u(self):
-        for k in (1, 3, 2):
-            self.back_v[k].arrived()
-        for k in (1, 3, 2):
-            self.back_u[k].start()
-
-    def return_c(self):
-        for k in (1, 3, 2):
-            self.back_u[k].arrived()
-        self.back_c.start()
+        mine = self.span(self.place.c)
+        both = self.part[mine] + self.half_in[...]
+        self.part[mine] = both
+        self.mid_out[...] = both.astype(BF16)
+        for message in self.out:
+            message.start()
+
+    def along_z(self):
+        total = self.part[self.span(self.place.c, self.mine)]
+        for k, message in enumerate(self.out):
+            message.arrived()
+            total = total + self.mid_in[k].astype(F32)
+        self.zed[self.z] = total
+        for message in self.by_z:
+            message.start()
+
+    def spread(self):
+        for message in self.by_z:
+            message.arrived()
+        total = (self.zed[0] + self.zed[1]) + (self.zed[2] + self.zed[3])
+        self.done[self.span(self.place.c, self.mine)] = total.astype(BF16)
+        for message in self.back:
+            message.start()
+
+    def swap(self):
+        for message in self.back:
+            message.arrived()
+        self.across.start()
 
     def last(self):
-        self.back_c.arrived()
+        self.across.arrived()
 
     def finish(self):
-        self.core.sent()
-        for group in (self.by_u, self.by_v, self.by_z, self.back_v, self.back_u):
-            for message in group.values():
-                message.sent()
-        self.back_c.sent()
-
-
-def half_out_dst(half_in):
-    return half_in
+        for message in (self.core, *self.out, *self.by_z, *self.back, self.across):
+            message.sent()
 
 
 def total_scratch(rows):
     return [
         pltpu.VMEM((rows, 128), F32),
+        pltpu.VMEM((rows // 2, 128), F32),
         pltpu.VMEM((rows // 2, 128), BF16),
-        pltpu.VMEM((rows // 2, 128), BF16),
-        pltpu.VMEM((rows // 2, 128), F32),
-        pltpu.VMEM((3, rows // 8, 128), BF16),
-        pltpu.VMEM((3, rows // 8, 128), BF16),
-        pltpu.VMEM((rows // 8, 128), F32),
-        pltpu.VMEM((3, rows // 32, 128), BF16),
-        pltpu.VMEM((3, rows // 32, 128), BF16),
-        pltpu.VMEM((4, rows // 32, 128), BF16),
-        pltpu.VMEM((rows, 128), BF16),
+        pltpu.VMEM((15, rows // 32, 128), BF16),
+        pltpu.VMEM((4, rows // 32, 128), F32),
     ]
 
 
@@ -374,15 +343,16 @@
 
 def kernel(
     feat, wqkv, wout, wconv, go,
-    gf, gqkv, gout, gconv,
-    feats, grads, stats, sib_feat, sib_grad, fine, rim,
+    gf, rest_done, qkv_done,
+    feats, grads, stats, sib_feat, sib_grad, fine, rim, sides,
     keys, values, qm, dm,
     scores, gweights, low_w, low_g, acc_a, acc_b,
     run_m, run_l, run_d, tri_out, tri_in,
     part_out, part_in, pair_out, pair_in, ghid, glow, gproj, hid,
-    *rest,
+    wide, *rest,
 ):
-    rest_total, qkv_total, (send, recv) = rest[:11], rest[11:22], rest[22:]
+    rest_total, qkv_total, (send, recv) = (*rest[:5], rest_done), (*rest[5:10], qkv_done), rest[10:12]
+    greet = rest[12]
     sems = (send, recv)
     place = Place()
     c, s, zl = place.c, place.s, place.zl
@@ -390,9 +360,9 @@
     above, below = place.line(-1), place.line(1)
 
     base = 0
-    fg = Gather(place, feats, sems, base)
+    fg = Gather(place, feats, sems, base, True)
     base += AG_MSGS
-    dg = Gather(place, grads, sems, base)
+    dg = Gather(place, grads, sems, base, False)
     base += AG_MSGS
     sg = StatGather(place, stats, sems, base)
     base += ST_MSGS
@@ -401,8 +371,8 @@
     qkv_sum = Total(place, QKV_ROWS, *qkv_total, sems, base)
     base += RS_MSGS
     sib_f = Message(feat, sib_feat, sib_feat, sems, base, sib)
-    down_fine = Message(fine.at[2], fine.at[0], fine.at[0], sems, base + 1, below)
-    up_fine = Message(fine.at[1], fine.at[3], fine.at[3], sems, base + 2, above)
+    down_fine = Message(go.at[1], fine.at[0], fine.at[0], sems, base + 1, below)
+    up_fine = Message(go.at[0], fine.at[1], fine.at[1], sems, base + 2, above)
     s0, f0 = place.coords(zl)
     own = (zl, s0, f0)
     sib_g = Message(grads.at[own], sib_grad, sib_grad, sems, base + 3, sib)
@@ -412,28 +382,50 @@
     up_hid = Message(hid, rim.at[1], rim.at[1], sems, base + 7, above)
     pairs = Message(pair_out, pair_in, pair_in, sems, base + 8, sib)
 
+    def scaled_queries(rows):
+        whole = nn(rows, wqkv[:, :CH]).astype(BF16)
+        return (whole.astype(F32) * (1.0 / math.sqrt(HDIM))).astype(BF16)
+
+    def stack_keys(rows, half):
+        whole = nn(rows, wqkv[:, CH:]).astype(BF16)
+        stack_heads(qm, half, whole[:, :CH])
+        stack_heads(dm, half, whole[:, CH:])
+
     barrier = pltpu.get_barrier_semaphore()
     peers = [sib, place.at(z=place.zo), above, below]
     peers += [place.ring_x(k) for k in (1, 2, 3)] + [place.ring_y(k) for k in (1, 2, 3)]
-    peers += [place.at(d=1 - place.d), place.at(d=1 - place.d, z=place.zo)]
+    next_z = place.at(d=1 - place.d, z=place.zo)
+    peers.append(next_z)
     for peer in peers:
         pl.semaphore_signal(barrier, inc=1, device_id=peer, device_id_type=MESH)
     pl.semaphore_wait(barrier, len(peers))
+    pl.semaphore_signal(greet, inc=1, device_id=next_z, device_id_type=MESH)
 
     feats[own] = feat[...]
-    fine[1] = go[0]
-    fine[2] = go[1]
     down_fine.start()
     up_fine.start()
     fg.begin()
     sib_f.start()
 
+    def split(rows, shift=False):
+        wide[...] = rows.astype(F32)
+        return wide[pl.ds(0, ROW, stride=2)], wide[pl.ds(1, ROW, stride=2)]
+
+    def pack(even, odd):
+        return jnp.concatenate([even, odd], axis=1).astype(BF16)
+
+    own_lines = []
+    for r in (0, 1):
+        even, odd = split(go[r])
+        sides[r] = jnp.concatenate([even, odd, moved(even, 1), moved(odd, -1)], axis=1).astype(BF16)
+        own_lines.append(pack(even, odd))
+    stack_heads(qm, 0, scaled_queries(feat[...]))
     down_fine.arrived()
     up_fine.arrived()
-    rows = fine[...]
-    top = jnp.where(s > 0, rows[0], jnp.zeros_like(rows[0]))
-    bottom = jnp.where(s < 63, rows[3], jnp.zeros_like(rows[3]))
-    lines = [top, rows[1], rows[2], bottom]
+    top, bottom = pack(*split(fine[0])), pack(*split(fine[1]))
+    top = jnp.where(s > 0, top, jnp.zeros_like(top))
+    bottom = jnp.where(s < 63, bottom, jnp.zeros_like(bottom))
+    lines = [top, *own_lines, bottom]
     main = jnp.zeros((2 * ROW, CH), F32)
     plus = jnp.zeros((2 * ROW, CH), F32)
     minus = jnp.zeros((2 * ROW, CH), F32)
@@ -451,24 +443,13 @@
     own_grad = nt(hidden_low, wout[...]).astype(BF16)
     grads[own] = own_grad
     sib_g.start()
+    dg.begin()
     fg.other()
     fg.near(0)
+    fg.far(0)
     fg.pass_on(0, 0)
-    dg.begin()
-
-    def scaled_queries(rows):
-        whole = nn(rows, wqkv[:, :CH]).astype(BF16)
-        return (whole.astype(F32) * (1.0 / math.sqrt(HDIM))).astype(BF16)
-
-    def stack_keys(rows, half):
-        whole = nn(rows, wqkv[:, CH:]).astype(BF16)
-        stack_heads(qm, half, whole[:, :CH])
-        stack_heads(dm, half, whole[:, CH:])
-
-    stack_heads(qm, 0, scaled_queries(feat[...]))
+
     stack_heads(dm, 0, own_grad)
-    fg.near(1)
-    fg.pass_on(1, 0)
     sib_f.arrived()
     stack_heads(qm, 1, scaled_queries(sib_feat[...]))
     sib_g.arrived()
@@ -479,9 +460,9 @@
     run_d[...] = jnp.zeros((STACK, 128), F32)
 
     def where_is(j):
-        role, order = lax.rem(j, 2), j // 2
+        role = jnp.where((j == 1) | (j == 4) | (j == 5) | (j == 7), 1, 0)
         t = jnp.where(role == 0, zl, place.zo)
-        offset = jnp.where(order == 0, 0, jnp.where(order == 1, 3, jnp.where(order == 2, 1, 2)))
+        offset = jnp.where(j < 2, 0, jnp.where(j > 5, 2, jnp.where(lax.rem(j, 2) == 0, 3, 1)))
         second, _ = place.coords(t)
         return t, lax.rem(second + offset, RING)
 
@@ -491,22 +472,23 @@
 
     def stat_steps():
         def first(j, unused):
-            def act0():
-                fg.far(0)
-
             def act1():
+                fg.near(1)
                 fg.far(1)
+                fg.pass_on(1, 0)
 
             def act2():
                 fg.pass_on(0, 1, 2, 3)
+
+            def act3():
                 dg.other()
-
-            def act3():
-                fg.pass_on(1, 1, 2, 3)
                 dg.near(0)
                 dg.pass_on(0, 0)
 
             def act4():
+                fg.pass_on(1, 1, 2, 3)
+
+            def act5():
                 dg.near(1)
                 dg.pass_on(1, 0)
 
@@ -518,7 +500,7 @@
                 fg.last(1)
                 dg.far(1)
 
-            at_step(j, {0: act0, 1: act1, 2: act2, 3: act3, 4: act4, 6: act6, 7: act7})
+            at_step(j, {1: act1, 2: act2, 3: act3, 4: act4, 5: act5, 6: act6, 7: act7})
             t, second = where_is(j)
             block = feats[t, second].reshape(CHUNK, CH)
             whole = nn(block, wqkv[:, CH:]).astype(BF16)
@@ -590,21 +572,21 @@
 
     def forward(j, unused):
         def act0():
+            dg.pass_on(0, 1, 2)
+
+        def act1():
             sg.other()
-            dg.pass_on(0, 1, 2)
-
-        def act1():
+
+        def act2():
             dg.pass_on(1, 1, 2)
-            sg.spread(0)
-
-        def act2():
+
+        def act3():
             dg.pass_on(0, 3)
-            sg.spread(1)
-
-        def act3():
+
+        def act4():
             dg.pass_on(1, 3)
 
-        at_step(j, {0: act0, 1: act1, 2: act2, 3: act3})
+        at_step(j, {0: act0, 1: act1, 2: act2, 3: act3, 4: act4})
 
         for half in (0, 1):
 
@@ -640,18 +622,16 @@
     out_part = tn(attended, glow[...])
     rest_sum.part[2304:2560] = out_part[:, :128]
     rest_sum.part[2560:2816] = out_part[:, 128:]
-    rest_sum.part[2816:] = jnp.zeros((REST_ROWS - 2816, 128), F32)
+    query_part = tn(feat[...], gproj[:, :CH])
+    rest_sum.part[2816:3072] = query_part[:, :128]
+    rest_sum.part[3072:3328] = query_part[:, 128:]
+    rest_sum.part[3328:] = jnp.zeros((REST_ROWS - 3328, 128), F32)
 
     down_hid.arrived()
     up_hid.arrived()
     mid = hid[...]
     over = jnp.where(s > 0, rim[0], jnp.zeros_like(mid))
     under = jnp.where(s < 63, rim[1], jnp.zeros_like(mid))
-    sides = []
-    for r in (0, 1):
-        wide = go[r].astype(F32)
-        even, odd = wide[:, :CO], wide[:, CO:]
-        sides.append(jnp.concatenate([even, odd, moved(even, 1), moved(odd, -1)], axis=1).astype(BF16))
     products = {
         (0, 0): tn(mid, sides[0]),
         (0, 1): tn(mid, sides[1]),
@@ -673,6 +653,7 @@
 
     stack_keys(feat[...], 0)
     stack_keys(sib_feat[...], 1)
+    pl.semaphore_wait(greet, 1)
     dg.last(0)
     dg.last(1)
     sg.last()
@@ -683,12 +664,8 @@
         at_step(
             j,
             {
-                1: rest_sum.step_u,
-                2: rest_sum.step_v,
-                3: rest_sum.step_z,
-                4: rest_sum.return_v,
-                5: rest_sum.return_u,
-                6: rest_sum.return_c,
+                1: rest_sum.scatter,
+                5: rest_sum.along_z,
             },
         )
         t, second = where_is(j)
@@ -727,26 +704,19 @@
     gproj[:, CH : 2 * CH] = (gk_mine + pair_in[:, :CH]).astype(BF16)
     gproj[:, 2 * CH :] = (gv_mine + pair_in[:, CH:]).astype(BF16)
     proj = gproj[...]
-    qkv_part = tn(feat[...], proj)
-    for k in range(6):
+    qkv_part = tn(feat[...], proj[:, CH:])
+    for k in range(4):
         qkv_sum.part[k * CH : (k + 1) * CH] = qkv_part[:, k * 128 : (k + 1) * 128]
     qkv_sum.begin()
+    rest_sum.spread()
+    qkv_sum.scatter()
     gf[...] = ghid[...] + nt(proj, wqkv[...])
-    coarse = 1.0 / math.sqrt(2 * 64 * ROW)
-    fine_scale = 1.0 / math.sqrt(2 * 128 * 256)
-    qkv_sum.step_u()
+    qkv_sum.along_z()
+    rest_sum.swap()
+    qkv_sum.spread()
     rest_sum.last()
-    gconv[...] = rest_sum.done[:2304].astype(F32) * fine_scale
-    gout[:, :128] = rest_sum.done[2304:2560].astype(F32) * coarse
-    gout[:, 128:] = rest_sum.done[2560:2816].astype(F32) * coarse
-    qkv_sum.step_v()
-    qkv_sum.step_z()
-    qkv_sum.return_v()
-    qkv_sum.return_u()
-    qkv_sum.return_c()
+    qkv_sum.swap()
     qkv_sum.last()
-    for k in range(6):
-        gqkv[:, k * 128 : (k + 1) * 128] = qkv_sum.done[k * CH : (k + 1) * CH].astype(F32) * coarse
 
     for group in (fg, dg, sg, rest_sum, qkv_sum):
         group.finish()
@@ -754,27 +724,39 @@
         message.sent()
 
 
+def scale_out(gf_in, rest, qkv, gf, gqkv, gout, gconv):
+    coarse = 1.0 / math.sqrt(2 * 64 * ROW)
+    fine_scale = 1.0 / math.sqrt(2 * 128 * 256)
+    gf[...] = gf_in[...]
+    gconv[...] = rest[:2304].astype(F32) * fine_scale
+    for k in range(2):
+        gout[:, k * 128 : (k + 1) * 128] = rest[2304 + k * CH : 2304 + (k + 1) * CH].astype(F32) * coarse
+        gqkv[:, k * 128 : (k + 1) * 128] = rest[2816 + k * CH : 2816 + (k + 1) * CH].astype(F32) * coarse
+    for k in range(4):
+        gqkv[:, CH + k * 128 : CH + (k + 1) * 128] = qkv[k * CH : (k + 1) * CH].astype(F32) * coarse
+
+
 def shards(features, qkv_weight, out_weight, conv_weight, grad_output):
     messages = 2 * AG_MSGS + ST_MSGS + 2 * RS_MSGS + 9
     whole = pl.BlockSpec(memory_space=pltpu.VMEM)
-    gf, gqkv, gout, gconv = pl.pallas_call(
+    sums = pl.pallas_call(
         kernel,
         out_shape=[
             jax.ShapeDtypeStruct((ROW, CH), F32),
-            jax.ShapeDtypeStruct((CH, 3 * CH), F32),
-            jax.ShapeDtypeStruct((CH, CH), F32),
-            jax.ShapeDtypeStruct((9 * CH, CO), F32),
+            jax.ShapeDtypeStruct((REST_ROWS, 128), BF16),
+            jax.ShapeDtypeStruct((QKV_ROWS, 128), BF16),
         ],
         in_specs=[whole] * 5,
-        out_specs=[whole] * 4,
+        out_specs=[whole] * 3,
         scratch_shapes=[
             pltpu.VMEM((2, RING, RING, ROW, CH), BF16),
             pltpu.VMEM((2, RING, RING, ROW, CH), BF16),
             pltpu.VMEM((2, RING, RING, 2 * HEADS, ROW), F32),
             pltpu.VMEM((ROW, CH), BF16),
             pltpu.VMEM((ROW, CH), BF16),
-            pltpu.VMEM((4, ROW, 2 * CO), BF16),
+            pltpu.VMEM((2, 2 * ROW, CO), BF16),
             pltpu.VMEM((2, ROW, CH), BF16),
+            pltpu.VMEM((2, ROW, 4 * CO), BF16),
             pltpu.VMEM((CHUNKS, CHUNK, CH), BF16),
             pltpu.VMEM((CHUNKS, CHUNK, CH), BF16),
             pltpu.VMEM((STACK, CH), BF16),
@@ -798,10 +780,12 @@
             pltpu.VMEM((ROW, CH), BF16),
             pltpu.VMEM((ROW, 3 * CH), BF16),
             pltpu.VMEM((ROW, CH), BF16),
+            pltpu.VMEM((2 * ROW, CO), F32),
             *total_scratch(REST_ROWS),
             *total_scratch(QKV_ROWS),
             pltpu.SemaphoreType.DMA((messages,)),
             pltpu.SemaphoreType.DMA((messages,)),
+            pltpu.SemaphoreType.REGULAR,
         ],
         compiler_params=pltpu.CompilerParams(
             collective_id=0, has_side_effects=True, vmem_limit_bytes=63 * 1024 * 1024
@@ -811,8 +795,20 @@
         qkv_weight,
         out_weight,
         conv_weight.reshape(9, CH, CO),
-        grad_output.reshape(2, ROW, 2 * CO),
+        grad_output.reshape(2, 2 * ROW, CO),
     )
+    gf, gqkv, gout, gconv = pl.pallas_call(
+        scale_out,
+        out_shape=[
+            jax.ShapeDtypeStruct((ROW, CH), F32),
+            jax.ShapeDtypeStruct((CH, 3 * CH), F32),
+            jax.ShapeDtypeStruct((CH, CH), F32),
+            jax.ShapeDtypeStruct((9 * CH, CO), F32),
+        ],
+        in_specs=[whole] * 3,
+        out_specs=[whole] * 4,
+        compiler_params=pltpu.CompilerParams(vmem_limit_bytes=16 * 1024 * 1024),
+    )(*sums)
     return (
         gf.reshape(1, 1, ROW, CH),
         gqkv,

time: 127 us -> 106 us (0.83)
  Pallas kernels: 119 us -> 102 us
  local copies, waits for them, and re-layouts: 7.07 us -> 3.03 us
    pallas_call x1, Pallas kernels: 119 us -> 100 us  [shards(): pl.pallas_call(kernel, out_shape=[jax.ShapeDtypeStruct((ROW, CH), F32), j...]
    unnamed x8 -> x6, local copies, waits for them, and re-layouts: 5.46 us -> 3.03 us
    reshape x1 -> x0, local copies, waits for them, and re-layouts: 1.61 us -> none  [shards(): grad_output.reshape(2, ROW, 2 * CO)]
    pallas_call x0 -> x1, Pallas kernels: none -> 1.48 us  [shards(): pl.pallas_call(scale_out, out_shape=[jax.ShapeDtypeStruct((ROW, CH), F32)...]
where the time goes in v2:
time: 106 us
  Pallas kernels  102 us (96%)
  local copies, waits for them, and re-layouts  3.03 us (3%)
    pallas_call x1, Pallas kernels, shards(): pl.pallas_call(kernel, out_shape=[jax.ShapeDtypeStruct((ROW, CH), F32), j...  100 us
    unnamed x6, local copies, waits for them, and re-layouts  3.03 us

profile of v2, /device:TPU:1, one launch (start us, length us, event | category | flops | bytes accessed | tf_op | source)
XLA Modules:
  0.0 105.6 jit_solution(7681084717986913853)
XLA Ops:
  0.6 100.4 %shard_map.84 = (f32[128,256]{1,0:T(8,128)}, bf16[3584,128]{1,0:T(8,128)(2,1)}, bf16[1024,128]{1,0:T(8,128)(2,1)}) custom-call(bf16[128,256]{1,0:T(8,128)(2,1)} %bitcast.7, bf16[256,768]{1,0:T(8,128)(2,1)} %wqkv.1, bf16[256,256]{1,0:T(8,128)(2,1)} %wout.1, bf16[9,256,128]{2,1,0:T(8,128)(2,1)} %bitcast.5, bf16[2,256,128]{2,1,0:T(8,128)(2,1)} %bitcast.6), custom_call_target="tpu_custom_call" | custom-call | tf_op jit(solution)/shard_map/pallas_call | solution.py:742
  101.1 0.0 copy-start
  101.1 1.2 %copy-done = bf16[3584,128]{1,0:T(8,128)(2,1)S(1)} copy-done((bf16[3584,128]{1,0:T(8,128)(2,1)S(1)}, bf16[3584,128]{1,0:T(8,128)(2,1)}, u32[]{:S(2)}) %copy-start) | copy-done | bytes 917528
  102.3 0.0 copy-start.1
  102.3 0.9 copy-done.1
  103.2 0.0 copy-start.2
  103.2 0.9 copy-done.2
  104.1 1.5 %shard_map.85 = (f32[128,256]{1,0:T(8,128)}, f32[256,768]{1,0:T(8,128)}, f32[256,256]{1,0:T(8,128)}, f32[2304,128]{1,0:T(8,128)}) custom-call(f32[128,256]{1,0:T(8,128)S(1)} %copy-done.2, bf16[3584,128]{1,0:T(8,128)(2,1)S(1)} %copy-done, bf16[1024,128]{1,0:T(8,128)(2,1)S(1)} %copy-done.1), custom_call_target="tpu_custom_call" | custom-call | tf_op jit(solution)/shard_map/pallas_call | solution.py:800
Async XLA Ops:
  101.1 1.2 %copy-start = (bf16[3584,128]{1,0:T(8,128)(2,1)S(1)}, bf16[3584,128]{1,0:T(8,128)(2,1)}, u32[]{:S(2)}) copy-start(bf16[3584,128]{1,0:T(8,128)(2,1)} %get-tuple-element.12.rest) | copy-start | bytes 2752516
  102.3 0.9 copy-start.1
  103.2 0.9 copy-start.2

commit v3 on v2

--- a/solution.py
+++ b/solution.py
@@ -19,8 +19,9 @@
 CHUNK = RING * ROW
 CHUNKS = 8
 STACK = 2 * HEADS * ROW
-HALF = STACK // 2
+PAIR = STACK // 2
 SUB = 32
+SLOT = RING * STACK
 REST_ROWS = 3584
 QKV_ROWS = 1024
 PLANE = [(k % 4, k // 4) for k in range(1, 16)]
@@ -306,7 +307,6 @@
 
 def total_scratch(rows):
     return [
-        pltpu.VMEM((rows, 128), F32),
         pltpu.VMEM((rows // 2, 128), F32),
         pltpu.VMEM((rows // 2, 128), BF16),
         pltpu.VMEM((15, rows // 32, 128), BF16),
@@ -321,16 +321,17 @@
 
 def stack_heads(ref, half, rows):
     for h in range(HEADS):
-        start = (half * HEADS + h) * ROW
+        start = ((h // 2) * 4 + half * 2 + h % 2) * ROW
         ref[start : start + ROW] = jnp.where(head_mask(rows.shape, h), rows, jnp.zeros_like(rows))
 
 
 def unstack_heads(ref, half):
-    out = jnp.zeros((ROW, CH), F32)
-    for h in range(HEADS):
-        start = (half * HEADS + h) * ROW
-        out = jnp.where(head_mask((ROW, CH), h), ref[start : start + ROW], out)
-    return out
+    out = []
+    for pair in range(2):
+        start = (pair * 4 + half * 2) * ROW
+        first, second = ref[start : start + ROW], ref[start + ROW : start + 2 * ROW]
+        out.append(jnp.where(head_mask((ROW, 128), 0), first, second))
+    return jnp.concatenate(out, axis=1)
 
 
 def moved(rows, step):
@@ -345,14 +346,15 @@
     feat, wqkv, wout, wconv, go,
     gf, rest_done, qkv_done,
     feats, grads, stats, sib_feat, sib_grad, fine, rim, sides,
-    keys, values, qm, dm,
-    scores, gweights, low_w, low_g, acc_a, acc_b,
+    keys, values, queries, qm, dm,
+    even, odd, low_w0, low_g0, low_w1, low_g1, acc_a, acc_b,
     run_m, run_l, run_d, tri_out, tri_in,
-    part_out, part_in, pair_out, pair_in, ghid, glow, gproj, hid,
+    part_out, part_in, kept, pair_out, pair_in, ghid, glow, gproj, hid,
     wide, *rest,
 ):
-    rest_total, qkv_total, (send, recv) = (*rest[:5], rest_done), (*rest[5:10], qkv_done), rest[10:12]
-    greet = rest[12]
+    rest_total = (odd.at[pl.ds(4 * SLOT, REST_ROWS)], *rest[:4], rest_done)
+    qkv_total = (odd.at[pl.ds(5 * SLOT, QKV_ROWS)], *rest[4:8], qkv_done)
+    send, recv, greet = rest[8:]
     sems = (send, recv)
     place = Place()
     c, s, zl = place.c, place.s, place.zl
@@ -398,44 +400,57 @@
     peers.append(next_z)
     for peer in peers:
         pl.semaphore_signal(barrier, inc=1, device_id=peer, device_id_type=MESH)
+
+    def split(rows):
+        wide[...] = rows.astype(F32)
+        return wide[pl.ds(0, ROW, stride=2)], wide[pl.ds(1, ROW, stride=2)]
+
+    def pack(*cells):
+        return jnp.concatenate(cells, axis=1).astype(BF16)
+
+    def taps(lines, a):
+        w0, w1, w2 = wconv[3 * a], wconv[3 * a + 1], wconv[3 * a + 2]
+        main = nt(lines, jnp.concatenate([w1, w0], axis=1)) + nt(lines, jnp.concatenate([w2, w1], axis=1))
+        return main, nt(lines[:, :CO], w0), nt(lines[:, CO:], w2)
+
+    feats[own] = feat[...]
+    stack_heads(qm, 0, scaled_queries(feat[...]))
+    own_lines = []
+    for r in (0, 1):
+        even_cells, odd_cells = split(go[r])
+        sides[r] = pack(even_cells, odd_cells, moved(even_cells, 1), moved(odd_cells, -1))
+        own_lines.append(pack(even_cells, odd_cells))
+    middle = taps(jnp.concatenate(own_lines, axis=0), 1)
+    local = [
+        m[:ROW] + m[ROW:] + f + l for m, f, l in zip(middle, taps(own_lines[1], 0), taps(own_lines[0], 2), strict=True)
+    ]
+    run_m[...] = jnp.full((STACK, 128), -1e30, F32)
+    run_l[...] = jnp.zeros((STACK, 128), F32)
+    run_d[...] = jnp.zeros((STACK, 128), F32)
+    odd[:SLOT] = jnp.full((SLOT, 128), -1e30, F32)
+    odd[SLOT : 2 * SLOT] = jnp.zeros((SLOT, 128), F32)
+
+    def clear():
+        for ref in (acc_a, acc_b):
+            ref[...] = jnp.zeros((STACK, 128), F32)
+        for ref in (low_w1, low_g1):
+            ref[...] = jnp.zeros((PAIR, CHUNK), BF16)
+
+    clear()
+
     pl.semaphore_wait(barrier, len(peers))
     pl.semaphore_signal(greet, inc=1, device_id=next_z, device_id_type=MESH)
-
-    feats[own] = feat[...]
     down_fine.start()
     up_fine.start()
     fg.begin()
     sib_f.start()
 
-    def split(rows, shift=False):
-        wide[...] = rows.astype(F32)
-        return wide[pl.ds(0, ROW, stride=2)], wide[pl.ds(1, ROW, stride=2)]
-
-    def pack(even, odd):
-        return jnp.concatenate([even, odd], axis=1).astype(BF16)
-
-    own_lines = []
-    for r in (0, 1):
-        even, odd = split(go[r])
-        sides[r] = jnp.concatenate([even, odd, moved(even, 1), moved(odd, -1)], axis=1).astype(BF16)
-        own_lines.append(pack(even, odd))
-    stack_heads(qm, 0, scaled_queries(feat[...]))
     down_fine.arrived()
     up_fine.arrived()
     top, bottom = pack(*split(fine[0])), pack(*split(fine[1]))
     top = jnp.where(s > 0, top, jnp.zeros_like(top))
     bottom = jnp.where(s < 63, bottom, jnp.zeros_like(bottom))
-    lines = [top, *own_lines, bottom]
-    main = jnp.zeros((2 * ROW, CH), F32)
-    plus = jnp.zeros((2 * ROW, CH), F32)
-    minus = jnp.zeros((2 * ROW, CH), F32)
-    for a in range(3):
-        both = jnp.concatenate([lines[2 - a], lines[3 - a]], axis=0)
-        w0, w1, w2 = wconv[3 * a], wconv[3 * a + 1], wconv[3 * a + 2]
-        main = main + nt(both, jnp.concatenate([w1, w0], axis=1)) + nt(both, jnp.concatenate([w2, w1], axis=1))
-        plus = plus + nt(both[:, :CO], w0)
-        minus = minus + nt(both[:, CO:], w2)
-    main, plus, minus = (m[:ROW] + m[ROW:] for m in (main, plus, minus))
+    main, plus, minus = (m + f + l for m, f, l in zip(local, taps(bottom, 0), taps(top, 2), strict=True))
     hidden_grad = main + moved(plus, 1) + moved(minus, -1)
     ghid[...] = hidden_grad
     hidden_low = hidden_grad.astype(BF16)
@@ -455,10 +470,6 @@
     sib_g.arrived()
     stack_heads(dm, 1, sib_grad[...])
 
-    run_m[...] = jnp.full((STACK, 128), -1e30, F32)
-    run_l[...] = jnp.zeros((STACK, 128), F32)
-    run_d[...] = jnp.zeros((STACK, 128), F32)
-
     def where_is(j):
         role = jnp.where((j == 1) | (j == 4) | (j == 5) | (j == 7), 1, 0)
         t = jnp.where(role == 0, zl, place.zo)
@@ -466,72 +477,89 @@
         second, _ = place.coords(t)
         return t, lax.rem(second + offset, RING)
 
-    def at_step(j, steps):
-        for when, act in steps.items():
-            pl.when(j == when)(act)
-
-    def stat_steps():
-        def first(j, unused):
-            def act1():
-                fg.near(1)
-                fg.far(1)
-                fg.pass_on(1, 0)
-
-            def act2():
-                fg.pass_on(0, 1, 2, 3)
-
-            def act3():
-                dg.other()
-                dg.near(0)
-                dg.pass_on(0, 0)
-
-            def act4():
-                fg.pass_on(1, 1, 2, 3)
-
-            def act5():
-                dg.near(1)
-                dg.pass_on(1, 0)
-
-            def act6():
-                fg.last(0)
-                dg.far(0)
-
-            def act7():
-                fg.last(1)
-                dg.far(1)
-
-            at_step(j, {1: act1, 2: act2, 3: act3, 4: act4, 5: act5, 6: act6, 7: act7})
+    def steps(jj, p, acts):
+        for when, act in acts.items():
+            if when % 2 == p:
+                pl.when(jj == when // 2)(act)
+
+    holds = (even, odd)
+    lows = ((low_w0, low_g0), (low_w1, low_g1))
+
+    def tile_at(slot, b, first, count):
+        return pl.ds(pl.multiple_of(slot * SLOT + b * STACK + first, SUB), count)
+
+    def put(ref, slot, pair, product):
+        for b in range(RING):
+            ref[tile_at(slot, b, pair * PAIR, PAIR)] = product[:, b * 128 : (b + 1) * 128]
+
+    def statistics(ref, slot, pair):
+        for i in range(PAIR // SUB):
+            first = pair * PAIR + i * SUB
+            span = slice(first, first + SUB)
+            sc = [ref[tile_at(slot, b, first, SUB)] for b in range(RING)]
+            old = run_m[span]
+            new = jnp.maximum(jnp.maximum(jnp.maximum(sc[0], sc[1]), jnp.maximum(sc[2], sc[3])), old)
+            shrink = jnp.exp(old - new)
+            total, dot = run_l[span] * shrink, run_d[span] * shrink
+            for b in range(RING):
+                w = jnp.exp(sc[b] - new)
+                total = total + w
+                dot = dot + w * ref[tile_at(slot + 1, b, first, SUB)]
+            run_m[span] = new
+            run_l[span] = total
+            run_d[span] = dot
+
+    def f1():
+        fg.near(1)
+        fg.far(1)
+        fg.pass_on(1, 0)
+
+    def f2():
+        fg.pass_on(0, 1, 2, 3)
+
+    def f3():
+        dg.other()
+        dg.near(0)
+        dg.pass_on(0, 0)
+
+    def f4():
+        fg.pass_on(1, 1, 2, 3)
+
+    def f5():
+        dg.near(1)
+        dg.pass_on(1, 0)
+
+    def f6():
+        fg.last(0)
+        dg.far(0)
+
+    def f7():
+        fg.last(1)
+        dg.far(1)
+
+    def first_pass(jj, skip):
+        for p in (0, 1):
+            j = 2 * jj + p
+            steps(jj, p, {1: f1, 2: f2, 3: f3, 4: f4, 5: f5, 6: f6, 7: f7})
             t, second = where_is(j)
             block = feats[t, second].reshape(CHUNK, CH)
-            whole = nn(block, wqkv[:, CH:]).astype(BF16)
-            keys[j] = whole[:, :CH]
-            values[j] = whole[:, CH:]
-            scores[j] = nt(qm[...], keys[j])
-            gweights[j] = nt(dm[...], values[j])
-
-            def tile(i, unused):
-                span = pl.ds(pl.multiple_of(i * SUB, SUB), SUB)
-                cut = [pl.ds(b * 128, 128) for b in range(RING)]
-                sc = [scores[j, span, k] for k in cut]
-                old = run_m[span]
-                new = jnp.maximum(jnp.maximum(jnp.maximum(sc[0], sc[1]), jnp.maximum(sc[2], sc[3])), old)
-                shrink = jnp.exp(old - new)
-                total, dot = run_l[span] * shrink, run_d[span] * shrink
-                for k in range(RING):
-                    w = jnp.exp(sc[k] - new)
-                    total = total + w
-                    dot = dot + w * gweights[j, span, cut[k]]
-                run_m[span] = new
-                run_l[span] = total
-                run_d[span] = dot
-                return unused
-
-            lax.fori_loop(0, STACK // SUB, tile, 0, unroll=4)
-            return unused
-
-        lax.fori_loop(0, CHUNKS, first, 0)
-
-    stat_steps()
+            whole = nn(block, wqkv[...]).astype(BF16)
+            queries[j] = (whole[:, :CH].astype(F32) * (1.0 / math.sqrt(HDIM))).astype(BF16)
+            keys[j] = whole[:, CH : 2 * CH]
+            values[j] = whole[:, 2 * CH :]
+            for pair in range(2):
+                rows = slice(pair * PAIR, (pair + 1) * PAIR)
+                put(holds[p], 2 * jj, pair, nt(qm[rows], whole[:, CH : 2 * CH]))
+                put(holds[p], 2 * jj + 1, pair, nt(dm[rows], whole[:, 2 * CH :]))
+                if p == 1:
+                    statistics(even, 2 * jj, pair)
+                else:
+                    statistics(odd, jnp.maximum(2 * jj - 2, 0), pair)
+        return skip
+
+    lax.fori_loop(0, CHUNKS // 2, first_pass, 0)
+    for pair in range(2):
+        statistics(odd, CHUNKS - 2, pair)
 
     lane = lax.broadcasted_iota(jnp.int32, (ROW, 128), 1)
     mine = [jnp.zeros((ROW, 128), F32), jnp.ones((ROW, 128), F32), jnp.zeros((ROW, 128), F32)]
@@ -539,7 +567,8 @@
     for half in (0, 1):
         for h in range(HEADS):
             g = half * HEADS + h
-            span = slice(g * ROW, (g + 1) * ROW)
+            start = ((h // 2) * 4 + half * 2 + h % 2) * ROW
+            span = slice(start, start + ROW)
             m = run_m[span]
             top = jnp.max(m, axis=1, keepdims=True)
             e = jnp.exp(m - top)
@@ -554,6 +583,8 @@
     for k in range(3):
         tri_out[k] = theirs[k]
     tri.start()
+    stack_keys(feat[...], 0)
+    stack_keys(sib_feat[...], 1)
     tri.arrived()
     top = jnp.maximum(mine[0], tri_in[0])
     ea, eb = jnp.exp(mine[0] - top), jnp.exp(tri_in[0] - top)
@@ -563,143 +594,156 @@
     stats[own] = jnp.concatenate([jnp.transpose(lse)[:HEADS], jnp.transpose(delta)[:HEADS]], axis=0)
     sg.begin()
     for g in range(2 * HEADS):
-        span = slice(g * ROW, (g + 1) * ROW)
+        half, h = g // HEADS, g % HEADS
+        start = ((h // 2) * 4 + half * 2 + h % 2) * ROW
+        span = slice(start, start + ROW)
         run_m[span] = jnp.broadcast_to(lse[:, g : g + 1], (ROW, 128))
         run_l[span] = jnp.broadcast_to(delta[:, g : g + 1], (ROW, 128))
 
-    acc_a[...] = jnp.zeros((STACK, CH), F32)
-    acc_b[...] = jnp.zeros((STACK, CH), F32)
-
-    def forward(j, unused):
-        def act0():
-            dg.pass_on(0, 1, 2)
-
-        def act1():
-            sg.other()
-
-        def act2():
-            dg.pass_on(1, 1, 2)
-
-        def act3():
-            dg.pass_on(0, 3)
-
-        def act4():
-            dg.pass_on(1, 3)
-
-        at_step(j, {0: act0, 1: act1, 2: act2, 3: act3, 4: act4})
-
-        for half in (0, 1):
-
-            def tile(i, unused, half=half):
-                own_span = pl.ds(pl.multiple_of(i * SUB, SUB), SUB)
-                span = pl.ds(pl.multiple_of(half * HALF + i * SUB, SUB), SUB)
-                lse_t, delta_t = run_m[span], run_l[span]
-                for b in range(RING):
-                    cut = pl.ds(b * 128, 128)
-                    w = jnp.exp(scores[j, span, cut] - lse_t)
-                    low_w[own_span, cut] = w.astype(BF16)
-                    low_g[own_span, cut] = (w * (gweights[j, span, cut] - delta_t)).astype(BF16)
-                return unused
-
-            lax.fori_loop(0, HALF // SUB, tile, 0, unroll=4)
-            into = slice(half * HALF, (half + 1) * HALF)
-            acc_a[into] += nn(low_w[...], values[j])
-            acc_b[into] += nn(low_g[...], keys[j])
-        return unused
-
-    lax.fori_loop(0, CHUNKS, forward, 0)
+    def weights_of(ref, p_slot, pair):
+        low_w, low_g = lows[pair]
+        for i in range(PAIR // SUB):
+            first = pair * PAIR + i * SUB
+            to = slice(i * SUB, (i + 1) * SUB)
+            lse_t, delta_t = run_m[first : first + SUB], run_l[first : first + SUB]
+            for b in range(RING):
+                w = jnp.exp(ref[tile_at(p_slot, b, first, SUB)] - lse_t)
+                low_w[to, b * 128 : (b + 1) * 128] = w.astype(BF16)
+                low_g[to, b * 128 : (b + 1) * 128] = (
+                    w * (ref[tile_at(p_slot + 1, b, first, SUB)] - delta_t)
+                ).astype(BF16)
+
+    def add_products(pair, with_w, with_g):
+        low_w, low_g = lows[pair]
+        rows = slice(pair * PAIR, (pair + 1) * PAIR)
+        acc_a[rows] += nn(low_w[...], with_w)
+        acc_b[rows] += nn(low_g[...], with_g)
+
+    def columns(pair):
+        return slice(pair * 128, (pair + 1) * 128)
+
+    def p0():
+        dg.pass_on(0, 1, 2)
+
+    def p1():
+        sg.other()
+
+    def p2():
+        dg.pass_on(1, 1, 2)
+
+    def p3():
+        dg.pass_on(0, 3)
+
+    def p4():
+        dg.pass_on(1, 3)
+
+    def forward(jj, skip):
+        for p in (0, 1):
+            j = 2 * jj + p
+            steps(jj, p, {0: p0, 1: p1, 2: p2, 3: p3, 4: p4})
+            before = jnp.maximum(j - 1, 0)
+            add_products(1, values[before, :, columns(1)], keys[before, :, columns(1)])
+            weights_of(holds[p], 2 * jj, 0)
+            add_products(0, values[j, :, columns(0)], keys[j, :, columns(0)])
+            weights_of(holds[p], 2 * jj, 1)
+        return skip
+
+    lax.fori_loop(0, CHUNKS // 2, forward, 0)
+    add_products(1, values[CHUNKS - 1, :, columns(1)], keys[CHUNKS - 1, :, columns(1)])
     part_out[0] = unstack_heads(acc_a, 1)
     part_out[1] = unstack_heads(acc_b, 1)
     parts.start()
-    attended_mine = unstack_heads(acc_a, 0)
-    gq_mine = unstack_heads(acc_b, 0)
-    parts.arrived()
-    attended = (attended_mine + part_in[0]).astype(BF16)
-    gproj[:, :CH] = ((gq_mine + part_in[1]) * (1.0 / math.sqrt(HDIM))).astype(BF16)
-    hid[...] = (feat[...].astype(F32) + nn(attended, wout[...])).astype(BF16)
-    down_hid.start()
-    up_hid.start()
-    out_part = tn(attended, glow[...])
-    rest_sum.part[2304:2560] = out_part[:, :128]
-    rest_sum.part[2560:2816] = out_part[:, 128:]
-    query_part = tn(feat[...], gproj[:, :CH])
-    rest_sum.part[2816:3072] = query_part[:, :128]
-    rest_sum.part[3072:3328] = query_part[:, 128:]
-    rest_sum.part[3328:] = jnp.zeros((REST_ROWS - 3328, 128), F32)
-
-    down_hid.arrived()
-    up_hid.arrived()
-    mid = hid[...]
-    over = jnp.where(s > 0, rim[0], jnp.zeros_like(mid))
-    under = jnp.where(s < 63, rim[1], jnp.zeros_like(mid))
-    products = {
-        (0, 0): tn(mid, sides[0]),
-        (0, 1): tn(mid, sides[1]),
-        (-1, 0): tn(over, sides[0]),
-        (1, 1): tn(under, sides[1]),
-    }
-    for a, whole in enumerate(
-        (
-            products[-1, 0] + products[0, 1],
-            products[0, 0] + products[0, 1],
-            products[0, 0] + products[1, 1],
-        )
-    ):
-        even, odd, even1, odd1 = (whole[:, k * CO : (k + 1) * CO] for k in range(4))
-        rest_sum.part[(3 * a) * CH : (3 * a + 1) * CH] = even1 + odd
-        rest_sum.part[(3 * a + 1) * CH : (3 * a + 2) * CH] = even + odd
-        rest_sum.part[(3 * a + 2) * CH : (3 * a + 3) * CH] = even + odd1
-    rest_sum.begin()
-
-    stack_keys(feat[...], 0)
-    stack_keys(sib_feat[...], 1)
+    kept[0] = unstack_heads(acc_a, 0)
+    kept[1] = unstack_heads(acc_b, 0)
+    clear()
+
+    def attended_rows():
+        parts.arrived()
+        attended = (kept[0] + part_in[0]).astype(BF16)
+        gproj[:, :CH] = ((kept[1] + part_in[1]) * (1.0 / math.sqrt(HDIM))).astype(BF16)
+        hid[...] = (feat[...].astype(F32) + nn(attended, wout[...])).astype(BF16)
+        down_hid.start()
+        up_hid.start()
+        out_part = tn(attended, glow[...])
+        part = rest_sum.part
+        part[2304:2560] = out_part[:, :128]
+        part[2560:2816] = out_part[:, 128:]
+        query_part = tn(feat[...], gproj[:, :CH])
+        part[2816:3072] = query_part[:, :128]
+        part[3072:3328] = query_part[:, 128:]
+        part[3328:] = jnp.zeros((REST_ROWS - 3328, 128), F32)
+
+    def conv_rows():
+        down_hid.arrived()
+        up_hid.arrived()
+        mid = hid[...]
+        over = jnp.where(s > 0, rim[0], jnp.zeros_like(mid))
+        under = jnp.where(s < 63, rim[1], jnp.zeros_like(mid))
+        same, other = tn(mid, sides[0]), tn(mid, sides[1])
+        part = rest_sum.part
+        for a, whole in enumerate((tn(over, sides[0]) + other, same + other, same + tn(under, sides[1]))):
+            even_c, odd_c, even1, odd1 = (whole[:, k * CO : (k + 1) * CO] for k in range(4))
+            part[(3 * a) * CH : (3 * a + 1) * CH] = even1 + odd_c
+            part[(3 * a + 1) * CH : (3 * a + 2) * CH] = even_c + odd_c
+            part[(3 * a + 2) * CH : (3 * a + 3) * CH] = even_c + odd1
+        rest_sum.begin()
+
+    def block_of(j):
+        t, second = where_is(j)
+        return grads[t, second].reshape(CHUNK, CH)
+
+    def transposed_scores(j, p, pair):
+        rows = slice(pair * PAIR, (pair + 1) * PAIR)
+        put(holds[p], 0, pair, nt(qm[rows], queries[j]))
+        put(holds[p], 1, pair, nt(dm[rows], block_of(j)))
+
+    def transposed_weights(j, p, pair):
+        low_w, low_g = lows[pair]
+        t, second = where_is(j)
+        for part in range(4):
+            h = 2 * pair + part % 2
+            for i in range(ROW // SUB):
+                first = part * ROW + i * SUB
+                to = slice(first, first + SUB)
+                for b in range(RING):
+                    w = jnp.exp(holds[p][tile_at(0, b, pair * PAIR + first, SUB)] - stats[t, second, b, h : h + 1, :])
+                    low_w[to, b * 128 : (b + 1) * 128] = w.astype(BF16)
+                    low_g[to, b * 128 : (b + 1) * 128] = (
+                        w * (holds[p][tile_at(1, b, pair * PAIR + first, SUB)] - stats[t, second, b, HEADS + h : HEADS + h + 1, :])
+                    ).astype(BF16)
+
+    def backward(jj, skip, final=False):
+        for p in (0, 1):
+            j = 2 * jj + p
+            if final and p == 0:
+                rest_sum.scatter()
+                dg.last(1)
+            if not final:
+                steps(jj, p, {2: attended_rows, 4: conv_rows, 5: lambda: dg.last(0)})
+            before = jnp.maximum(j - 1, 0)
+            more = not (final and p == 1)
+            if more:
+                transposed_scores(j + 1, 1 - p, 0)
+            add_products(1, block_of(before)[:, columns(1)], queries[before, :, columns(1)])
+            transposed_weights(j, p, 0)
+            if more:
+                transposed_scores(j + 1, 1 - p, 1)
+            add_products(0, block_of(j)[:, columns(0)], queries[j, :, columns(0)])
+            transposed_weights(j, p, 1)
+        return skip
+
     pl.semaphore_wait(greet, 1)
-    dg.last(0)
-    dg.last(1)
+    transposed_scores(0, 0, 0)
+    transposed_scores(0, 0, 1)
     sg.last()
-    acc_a[...] = jnp.zeros((STACK, CH), F32)
-    acc_b[...] = jnp.zeros((STACK, CH), F32)
-
-    def backward(j, unused):
-        at_step(
-            j,
-            {
-                1: rest_sum.scatter,
-                5: rest_sum.along_z,
-            },
-        )
-        t, second = where_is(j)
-        block = grads[t, second].reshape(CHUNK, CH)
-        asked = scaled_queries(feats[t, second].reshape(CHUNK, CH))
-        scores[0] = nt(qm[...], asked)
-        gweights[0] = nt(dm[...], block)
-        for half in (0, 1):
-            for h in range(HEADS):
-
-                def tile(i, unused, h=h, half=half):
-                    own_span = pl.ds(pl.multiple_of(h * ROW + i * SUB, SUB), SUB)
-                    span = pl.ds(pl.multiple_of((half * HEADS + h) * ROW + i * SUB, SUB), SUB)
-                    for b in range(RING):
-                        cut = pl.ds(b * 128, 128)
-                        w = jnp.exp(scores[0, span, cut] - stats[t, second, b, h : h + 1, :])
-                        low_w[own_span, cut] = w.astype(BF16)
-                        low_g[own_span, cut] = (
-                            w * (gweights[0, span, cut] - stats[t, second, b, HEADS + h : HEADS + h + 1, :])
-                        ).astype(BF16)
-                    return unused
-
-                lax.fori_loop(0, ROW // SUB, tile, 0, unroll=4)
-            into = slice(half * HALF, (half + 1) * HALF)
-            acc_a[into] += nn(low_g[...], asked)
-            acc_b[into] += nn(low_w[...], block)
-        return unused
-
-    lax.fori_loop(0, CHUNKS, backward, 0)
-    pair_out[:, :CH] = unstack_heads(acc_a, 1)
-    pair_out[:, CH:] = unstack_heads(acc_b, 1)
+    lax.fori_loop(0, CHUNKS // 2 - 1, backward, 0)
+    backward(CHUNKS // 2 - 1, 0, True)
+    add_products(1, block_of(CHUNKS - 1)[:, columns(1)], queries[CHUNKS - 1, :, columns(1)])
+    pair_out[:, :CH] = unstack_heads(acc_b, 1)
+    pair_out[:, CH:] = unstack_heads(acc_a, 1)
     pairs.start()
-    gk_mine = unstack_heads(acc_a, 0)
-    gv_mine = unstack_heads(acc_b, 0)
+    gk_mine = unstack_heads(acc_b, 0)
+    gv_mine = unstack_heads(acc_a, 0)
     pairs.arrived()
     gproj[:, CH : 2 * CH] = (gk_mine + pair_in[:, :CH]).astype(BF16)
     gproj[:, 2 * CH :] = (gv_mine + pair_in[:, CH:]).astype(BF16)
@@ -708,14 +752,15 @@
     for k in range(4):
         qkv_sum.part[k * CH : (k + 1) * CH] = qkv_part[:, k * 128 : (k + 1) * 128]
     qkv_sum.begin()
+    gf[...] = ghid[...] + nt(proj, wqkv[...])
+    qkv_sum.scatter()
+    rest_sum.along_z()
+    qkv_sum.along_z()
     rest_sum.spread()
-    qkv_sum.scatter()
-    gf[...] = ghid[...] + nt(proj, wqkv[...])
-    qkv_sum.along_z()
+    qkv_sum.spread()
     rest_sum.swap()
-    qkv_sum.spread()
+    qkv_sum.swap()
     rest_sum.last()
-    qkv_sum.swap()
     qkv_sum.last()
 
     for group in (fg, dg, sg, rest_sum, qkv_sum):
@@ -759,19 +804,23 @@
             pltpu.VMEM((2, ROW, 4 * CO), BF16),
             pltpu.VMEM((CHUNKS, CHUNK, CH), BF16),
             pltpu.VMEM((CHUNKS, CHUNK, CH), BF16),
+            pltpu.VMEM((CHUNKS, CHUNK, CH), BF16),
             pltpu.VMEM((STACK, CH), BF16),
             pltpu.VMEM((STACK, CH), BF16),
-            pltpu.VMEM((CHUNKS, STACK, CHUNK), F32),
-            pltpu.VMEM((CHUNKS, STACK, CHUNK), F32),
-            pltpu.VMEM((HALF, CHUNK), BF16),
-            pltpu.VMEM((HALF, CHUNK), BF16),
-            pltpu.VMEM((STACK, CH), F32),
-            pltpu.VMEM((STACK, CH), F32),
+            pltpu.VMEM((CHUNKS * SLOT, 128), F32),
+            pltpu.VMEM((CHUNKS * SLOT, 128), F32),
+            pltpu.VMEM((PAIR, CHUNK), BF16),
+            pltpu.VMEM((PAIR, CHUNK), BF16),
+            pltpu.VMEM((PAIR, CHUNK), BF16),
+            pltpu.VMEM((PAIR, CHUNK), BF16),
+            pltpu.VMEM((STACK, 128), F32),
+            pltpu.VMEM((STACK, 128), F32),
             pltpu.VMEM((STACK, 128), F32),
             pltpu.VMEM((STACK, 128), F32),
             pltpu.VMEM((STACK, 128), F32),
             pltpu.VMEM((3, ROW, 128), F32),
             pltpu.VMEM((3, ROW, 128), F32),
+            pltpu.VMEM((2, ROW, CH), F32),
             pltpu.VMEM((2, ROW, CH), F32),
             pltpu.VMEM((2, ROW, CH), F32),
             pltpu.VMEM((ROW, 2 * CH), F32),
@@ -807,7 +856,7 @@
         ],
         in_specs=[whole] * 3,
         out_specs=[whole] * 4,
-        compiler_params=pltpu.CompilerParams(vmem_limit_bytes=16 * 1024 * 1024),
+        compiler_params=pltpu.CompilerParams(vmem_limit_bytes=62 * 1024 * 1024),
     )(*sums)
     return (
         gf.reshape(1, 1, ROW, CH),

time: 106 us -> 87.7 us (0.83)
  Pallas kernels: 102 us -> 86.9 us
  local copies, waits for them, and re-layouts: 3.03 us -> 0 us
    pallas_call x1, Pallas kernels: 100 us -> 84.2 us  [shards(): pl.pallas_call(kernel, out_shape=[jax.ShapeDtypeStruct((ROW, CH), F32), j...]
    unnamed x6 -> x0, local copies, waits for them, and re-layouts: 3.03 us -> none
    pallas_call x1, Pallas kernels: 1.48 us -> 2.7 us  [shards(): pl.pallas_call(scale_out, out_shape=[jax.ShapeDtypeStruct((ROW, CH), F32)...]
where the time goes in v3:
time: 87.7 us; the launch traced here: 87.6 us
  Pallas kernels  86.9 us (99%)
    pallas_call x1, Pallas kernels, shards(): pl.pallas_call(kernel, out_shape=[jax.ShapeDtypeStruct((ROW, CH), F32), j...  84.2 us
    pallas_call x1, Pallas kernels, shards(): pl.pallas_call(scale_out, out_shape=[jax.ShapeDtypeStruct((ROW, CH), F32)...  2.7 us

profile of v3, /device:TPU:1, one launch (start us, length us, event | category | flops | bytes accessed | tf_op | source)
XLA Modules:
  0.0 87.6 jit_solution(2853211955648823791)
XLA Ops:
  0.6 84.2 %shard_map.84 = (f32[128,256]{1,0:T(8,128)}, bf16[3584,128]{1,0:T(8,128)(2,1)}, bf16[1024,128]{1,0:T(8,128)(2,1)}) custom-call(bf16[128,256]{1,0:T(8,128)(2,1)} %bitcast.7, bf16[256,768]{1,0:T(8,128)(2,1)} %wqkv.1, bf16[256,256]{1,0:T(8,128)(2,1)} %wout.1, bf16[9,256,128]{2,1,0:T(8,128)(2,1)} %bitcast.5, bf16[2,256,128]{2,1,0:T(8,128)(2,1)} %bitcast.6), custom_call_target="tpu_custom_call" | custom-call | tf_op jit(solution)/shard_map/pallas_call | solution.py:787
  84.9 2.7 %shard_map.85 = (f32[128,256]{1,0:T(8,128)}, f32[256,768]{1,0:T(8,128)}, f32[256,256]{1,0:T(8,128)}, f32[2304,128]{1,0:T(8,128)}) custom-call(f32[128,256]{1,0:T(8,128)} %get-tuple-element.11.gf_in, bf16[3584,128]{1,0:T(8,128)(2,1)} %get-tuple-element.12.rest, bf16[1024,128]{1,0:T(8,128)(2,1)} %get-tuple-element.13.qkv), custom_call_target="tpu_custom_call" | custom-call | tf_op jit(solution)/shard_map/pallas_call | solution.py:849

commit v4 on v3

--- a/solution.py
+++ b/solution.py
@@ -28,6 +28,7 @@
 AG_MSGS = 41
 ST_MSGS = 31
 RS_MSGS = 35
+WIDE_MSGS = 49
 
 
 def nt(a, b):
@@ -90,8 +91,8 @@
     def ring_y(self, step):
         return self.at(y=lax.rem(self.y + step + RING, RING))
 
-    def plane(self, dx, dy, z=None):
-        return self.at(x=lax.rem(self.x + dx + RING, RING), y=lax.rem(self.y + dy + RING, RING), z=z)
+    def plane(self, dx, dy, c=None):
+        return self.at(x=lax.rem(self.x + dx + RING, RING), y=lax.rem(self.y + dy + RING, RING), c=c)
 
     def back(self, t, dx, dy):
         x, y = lax.rem(self.x + RING - dx, RING), lax.rem(self.y + RING - dy, RING)
@@ -228,7 +229,7 @@
 
 
 class Total:
-    def __init__(self, place, rows, part, half_in, mid_out, mid_in, zed, done, sems, base):
+    def __init__(self, place, rows, part, half_in, mid_out, mid_in, zed, done, sems, base, wide):
         self.place, self.part, self.half_in = place, part, half_in
         self.mid_out, self.mid_in, self.zed, self.done = mid_out, mid_in, zed, done
         self.half, self.piece = rows // 2, rows // 32
@@ -236,9 +237,12 @@
         self.mine = place.y * RING + place.x
         self.z = place.d * 2 + place.zl
         sib = place.at(c=1 - c)
-        away = part.at[self.span(1 - c)]
-        self.core = Message(away, half_in, half_in, sems, base, sib)
-        slot = base + 1
+        slot = base
+        self.core = []
+        if not wide:
+            away = part.at[self.span(1 - c)]
+            self.core.append(Message(away, half_in, half_in, sems, slot, sib))
+            slot += 1
         self.out, self.by_z, self.back = [], [], []
         here = done.at[self.span(c, self.mine)]
         for k, (dx, dy) in enumerate(PLANE):
@@ -246,17 +250,24 @@
             src = mid_out.at[pl.ds(pl.multiple_of((y * RING + x) * self.piece, 16), self.piece)]
             self.out.append(Message(src, mid_in.at[k], mid_in.at[k], sems, slot, place.plane(dx, dy)))
             x, y = lax.rem(place.x + RING - dx, RING), lax.rem(place.y + RING - dy, RING)
-            self.back.append(
-                Message(here, here, done.at[self.span(c, y * RING + x)], sems, slot + 1, place.plane(dx, dy))
-            )
+            landing = done.at[self.span(c, y * RING + x)]
+            self.back.append(Message(here, here, landing, sems, slot + 1, place.plane(dx, dy)))
             slot += 2
+            if wide:
+                landing = done.at[self.span(1 - c, y * RING + x)]
+                self.back.append(Message(here, here, landing, sems, slot, place.plane(dx, dy, 1 - c)))
+                slot += 1
         for k in (1, 3, 2):
             to, of = lax.rem(self.z + k, 4), lax.rem(self.z + 4 - k, 4)
             src = zed.at[self.z]
             self.by_z.append(Message(src, src, zed.at[of], sems, slot, place.at(d=to // 2, z=lax.rem(to, 2))))
             slot += 1
-        src = done.at[self.span(c)]
-        self.across = Message(src, src, done.at[self.span(1 - c)], sems, slot, sib)
+        self.across = []
+        if wide:
+            self.back.append(Message(here, here, done.at[self.span(1 - c, self.mine)], sems, slot, sib))
+        else:
+            src = done.at[self.span(c)]
+            self.across.append(Message(src, src, done.at[self.span(1 - c)], sems, slot, sib))
 
     def span(self, c, piece=None):
         if piece is None:
@@ -264,12 +275,13 @@
         return pl.ds(pl.multiple_of(c * self.half + piece * self.piece, 16), self.piece)
 
     def begin(self):
-        self.core.start()
-
-    def scatter(self):
-        self.core.arrived()
+        self.core[0].start()
+
+    def scatter(self, both=None):
         mine = self.span(self.place.c)
-        both = self.part[mine] + self.half_in[...]
+        if both is None:
+            self.core[0].arrived()
+            both = self.part[mine] + self.half_in[...]
         self.part[mine] = both
         self.mid_out[...] = both.astype(BF16)
         for message in self.out:
@@ -295,13 +307,15 @@
     def swap(self):
         for message in self.back:
             message.arrived()
-        self.across.start()
+        for message in self.across:
+            message.start()
 
     def last(self):
-        self.across.arrived()
+        for message in self.across:
+            message.arrived()
 
     def finish(self):
-        for message in (self.core, *self.out, *self.by_z, *self.back, self.across):
+        for message in (*self.core, *self.out, *self.by_z, *self.back, *self.across):
             message.sent()
 
 
@@ -320,9 +334,11 @@
 
 
 def stack_heads(ref, half, rows):
-    for h in range(HEADS):
-        start = ((h // 2) * 4 + half * 2 + h % 2) * ROW
-        ref[start : start + ROW] = jnp.where(head_mask(rows.shape, h), rows, jnp.zeros_like(rows))
+    for pair in range(2):
+        cols = rows[:, pair * 128 : (pair + 1) * 128]
+        for h in range(2):
+            start = (pair * 4 + half * 2 + h) * ROW
+            ref[start : start + ROW] = jnp.where(head_mask(cols.shape, h), cols, jnp.zeros_like(cols))
 
 
 def unstack_heads(ref, half):
@@ -345,11 +361,11 @@
 def kernel(
     feat, wqkv, wout, wconv, go,
     gf, rest_done, qkv_done,
-    feats, grads, stats, sib_feat, sib_grad, fine, rim, sides,
+    feats, grads, stats, sib_feat, sib_grad, fine, sides,
     keys, values, queries, qm, dm,
     even, odd, low_w0, low_g0, low_w1, low_g1, acc_a, acc_b,
     run_m, run_l, run_d, tri_out, tri_in,
-    part_out, part_in, kept, pair_out, pair_in, ghid, glow, gproj, hid,
+    part_out, part_in, kept, pair_out, pair_in, gone_out, gone_in, ghid, glow, gproj, hid,
     wide, *rest,
 ):
     rest_total = (odd.at[pl.ds(4 * SLOT, REST_ROWS)], *rest[:4], rest_done)
@@ -368,10 +384,10 @@
     base += AG_MSGS
     sg = StatGather(place, stats, sems, base)
     base += ST_MSGS
-    rest_sum = Total(place, REST_ROWS, *rest_total, sems, base)
+    rest_sum = Total(place, REST_ROWS, *rest_total, sems, base, False)
     base += RS_MSGS
-    qkv_sum = Total(place, QKV_ROWS, *qkv_total, sems, base)
-    base += RS_MSGS
+    qkv_sum = Total(place, QKV_ROWS, *qkv_total, sems, base, True)
+    base += WIDE_MSGS
     sib_f = Message(feat, sib_feat, sib_feat, sems, base, sib)
     down_fine = Message(go.at[1], fine.at[0], fine.at[0], sems, base + 1, below)
     up_fine = Message(go.at[0], fine.at[1], fine.at[1], sems, base + 2, above)
@@ -380,9 +396,8 @@
     sib_g = Message(grads.at[own], sib_grad, sib_grad, sems, base + 3, sib)
     tri = Message(tri_out, tri_in, tri_in, sems, base + 4, sib)
     parts = Message(part_out, part_in, part_in, sems, base + 5, sib)
-    down_hid = Message(hid, rim.at[0], rim.at[0], sems, base + 6, below)
-    up_hid = Message(hid, rim.at[1], rim.at[1], sems, base + 7, above)
     pairs = Message(pair_out, pair_in, pair_in, sems, base + 8, sib)
+    final_rows = Message(gone_out, gone_in, gone_in, sems, base + 9, sib)
 
     def scaled_queries(rows):
         whole = nn(rows, wqkv[:, :CH]).astype(BF16)
@@ -414,11 +429,18 @@
         return main, nt(lines[:, :CO], w0), nt(lines[:, CO:], w2)
 
     feats[own] = feat[...]
+    pl.semaphore_wait(barrier, len(peers))
+    pl.semaphore_signal(greet, inc=1, device_id=next_z, device_id_type=MESH)
+    down_fine.start()
+    up_fine.start()
+    fg.begin()
+    sib_f.start()
+
     stack_heads(qm, 0, scaled_queries(feat[...]))
     own_lines = []
     for r in (0, 1):
         even_cells, odd_cells = split(go[r])
-        sides[r] = pack(even_cells, odd_cells, moved(even_cells, 1), moved(odd_cells, -1))
+        sides[1 + r] = pack(even_cells, odd_cells, moved(even_cells, 1), moved(odd_cells, -1))
         own_lines.append(pack(even_cells, odd_cells))
     middle = taps(jnp.concatenate(own_lines, axis=0), 1)
     local = [
@@ -438,18 +460,19 @@
 
     clear()
 
-    pl.semaphore_wait(barrier, len(peers))
-    pl.semaphore_signal(greet, inc=1, device_id=next_z, device_id_type=MESH)
-    down_fine.start()
-    up_fine.start()
-    fg.begin()
-    sib_f.start()
+    fg.other()
+    fg.near(0)
+    fg.far(0)
+    fg.pass_on(0, 0)
 
     down_fine.arrived()
     up_fine.arrived()
-    top, bottom = pack(*split(fine[0])), pack(*split(fine[1]))
-    top = jnp.where(s > 0, top, jnp.zeros_like(top))
-    bottom = jnp.where(s < 63, bottom, jnp.zeros_like(bottom))
+    outer = []
+    for r, inside in ((0, s > 0), (1, s < 63)):
+        even_cells, odd_cells = (jnp.where(inside, cells, 0.0) for cells in split(fine[r]))
+        sides[3 * r] = pack(even_cells, odd_cells, moved(even_cells, 1), moved(odd_cells, -1))
+        outer.append(pack(even_cells, odd_cells))
+    top, bottom = outer
     main, plus, minus = (m + f + l for m, f, l in zip(local, taps(bottom, 0), taps(top, 2), strict=True))
     hidden_grad = main + moved(plus, 1) + moved(minus, -1)
     ghid[...] = hidden_grad
@@ -459,10 +482,6 @@
     grads[own] = own_grad
     sib_g.start()
     dg.begin()
-    fg.other()
-    fg.near(0)
-    fg.far(0)
-    fg.pass_on(0, 0)
 
     stack_heads(dm, 0, own_grad)
     sib_f.arrived()
@@ -471,9 +490,9 @@
     stack_heads(dm, 1, sib_grad[...])
 
     def where_is(j):
-        role = jnp.where((j == 1) | (j == 4) | (j == 5) | (j == 7), 1, 0)
-        t = jnp.where(role == 0, zl, place.zo)
-        offset = jnp.where(j < 2, 0, jnp.where(j > 5, 2, jnp.where(lax.rem(j, 2) == 0, 3, 1)))
+        t = jnp.where((j == 1) | (j > 4), place.zo, zl)
+        far = (j == 4) | (j == 7)
+        offset = jnp.where(j < 2, 0, jnp.where(far, 2, jnp.where((j == 2) | (j == 5), 3, 1)))
         second, _ = place.coords(t)
         return t, lax.rem(second + offset, RING)
 
@@ -516,22 +535,24 @@
 
     def f2():
         fg.pass_on(0, 1, 2, 3)
+        dg.other()
 
     def f3():
-        dg.other()
         dg.near(0)
         dg.pass_on(0, 0)
 
     def f4():
-        fg.pass_on(1, 1, 2, 3)
+        fg.pass_on(1, 1, 2)
+        fg.last(0)
 
     def f5():
+        fg.pass_on(1, 3)
         dg.near(1)
         dg.pass_on(1, 0)
 
     def f6():
-        fg.last(0)
         dg.far(0)
+        dg.pass_on(0, 1, 2)
 
     def f7():
         fg.last(1)
@@ -549,8 +570,9 @@
             values[j] = whole[:, 2 * CH :]
             for pair in range(2):
                 rows = slice(pair * PAIR, (pair + 1) * PAIR)
-                put(holds[p], 2 * jj, pair, nt(qm[rows], whole[:, CH : 2 * CH]))
-                put(holds[p], 2 * jj + 1, pair, nt(dm[rows], whole[:, 2 * CH :]))
+                first = CH + pair * 128
+                put(holds[p], 2 * jj, pair, nt(qm[rows], whole[:, first : first + 128]))
+                put(holds[p], 2 * jj + 1, pair, nt(dm[rows], whole[:, first + CH : first + CH + 128]))
                 if p == 1:
                     statistics(even, 2 * jj, pair)
                 else:
@@ -623,24 +645,21 @@
         return slice(pair * 128, (pair + 1) * 128)
 
     def p0():
-        dg.pass_on(0, 1, 2)
+        dg.pass_on(1, 1, 2)
 
     def p1():
+        dg.pass_on(0, 3)
+
+    def p2():
         sg.other()
 
-    def p2():
-        dg.pass_on(1, 1, 2)
-
     def p3():
-        dg.pass_on(0, 3)
-
-    def p4():
         dg.pass_on(1, 3)
 
     def forward(jj, skip):
         for p in (0, 1):
             j = 2 * jj + p
-            steps(jj, p, {0: p0, 1: p1, 2: p2, 3: p3, 4: p4})
+            steps(jj, p, {0: p0, 1: p1, 2: p2, 3: p3})
             before = jnp.maximum(j - 1, 0)
             add_products(1, values[before, :, columns(1)], keys[before, :, columns(1)])
             weights_of(holds[p], 2 * jj, 0)
@@ -662,8 +681,6 @@
         attended = (kept[0] + part_in[0]).astype(BF16)
         gproj[:, :CH] = ((kept[1] + part_in[1]) * (1.0 / math.sqrt(HDIM))).astype(BF16)
         hid[...] = (feat[...].astype(F32) + nn(attended, wout[...])).astype(BF16)
-        down_hid.start()
-        up_hid.start()
         out_part = tn(attended, glow[...])
         part = rest_sum.part
         part[2304:2560] = out_part[:, :128]
@@ -674,14 +691,10 @@
         part[3328:] = jnp.zeros((REST_ROWS - 3328, 128), F32)
 
     def conv_rows():
-        down_hid.arrived()
-        up_hid.arrived()
         mid = hid[...]
-        over = jnp.where(s > 0, rim[0], jnp.zeros_like(mid))
-        under = jnp.where(s < 63, rim[1], jnp.zeros_like(mid))
-        same, other = tn(mid, sides[0]), tn(mid, sides[1])
+        met = [tn(mid, sides[r]) for r in range(4)]
         part = rest_sum.part
-        for a, whole in enumerate((tn(over, sides[0]) + other, same + other, same + tn(under, sides[1]))):
+        for a, whole in enumerate((met[2] + met[3], met[1] + met[2], met[0] + met[1])):
             even_c, odd_c, even1, odd1 = (whole[:, k * CO : (k + 1) * CO] for k in range(4))
             part[(3 * a) * CH : (3 * a + 1) * CH] = even1 + odd_c
             part[(3 * a + 1) * CH : (3 * a + 2) * CH] = even_c + odd_c
@@ -694,8 +707,8 @@
 
     def transposed_scores(j, p, pair):
         rows = slice(pair * PAIR, (pair + 1) * PAIR)
-        put(holds[p], 0, pair, nt(qm[rows], queries[j]))
-        put(holds[p], 1, pair, nt(dm[rows], block_of(j)))
+        put(holds[p], 0, pair, nt(qm[rows], queries[j, :, columns(pair)]))
+        put(holds[p], 1, pair, nt(dm[rows], block_of(j)[:, columns(pair)]))
 
     def transposed_weights(j, p, pair):
         low_w, low_g = lows[pair]
@@ -712,14 +725,22 @@
                         w * (holds[p][tile_at(1, b, pair * PAIR + first, SUB)] - stats[t, second, b, HEADS + h : HEADS + h + 1, :])
                     ).astype(BF16)
 
+    def first_sums():
+        attended_rows()
+        conv_rows()
+
+    def before_four():
+        dg.last(0)
+
     def backward(jj, skip, final=False):
         for p in (0, 1):
             j = 2 * jj + p
             if final and p == 0:
-                rest_sum.scatter()
                 dg.last(1)
+            if final and p == 1:
+                rest_sum.along_z()
             if not final:
-                steps(jj, p, {2: attended_rows, 4: conv_rows, 5: lambda: dg.last(0)})
+                steps(jj, p, {0: first_sums, 2: rest_sum.scatter, 3: before_four})
             before = jnp.maximum(j - 1, 0)
             more = not (final and p == 1)
             if more:
@@ -739,33 +760,33 @@
     lax.fori_loop(0, CHUNKS // 2 - 1, backward, 0)
     backward(CHUNKS // 2 - 1, 0, True)
     add_products(1, block_of(CHUNKS - 1)[:, columns(1)], queries[CHUNKS - 1, :, columns(1)])
-    pair_out[:, :CH] = unstack_heads(acc_b, 1)
-    pair_out[:, CH:] = unstack_heads(acc_a, 1)
+    first_core = c == 0
+    own_part = []
+    for half in (0, 1):
+        gk, gv = unstack_heads(acc_b, half), unstack_heads(acc_a, half)
+        pair_out[1 - half] = jnp.where(first_core, gv, gk)
+        own_part.append(jnp.where(first_core, gk, gv))
     pairs.start()
-    gk_mine = unstack_heads(acc_b, 0)
-    gv_mine = unstack_heads(acc_a, 0)
     pairs.arrived()
-    gproj[:, CH : 2 * CH] = (gk_mine + pair_in[:, :CH]).astype(BF16)
-    gproj[:, 2 * CH :] = (gv_mine + pair_in[:, CH:]).astype(BF16)
-    proj = gproj[...]
-    qkv_part = tn(feat[...], proj[:, CH:])
-    for k in range(4):
-        qkv_sum.part[k * CH : (k + 1) * CH] = qkv_part[:, k * 128 : (k + 1) * 128]
-    qkv_sum.begin()
-    gf[...] = ghid[...] + nt(proj, wqkv[...])
-    qkv_sum.scatter()
-    rest_sum.along_z()
+    done_rows = [(own_part[half] + pair_in[half]).astype(BF16) for half in (0, 1)]
+    gone_out[...] = done_rows[1]
+    final_rows.start()
+    qkv_part = tn(jnp.concatenate([feat[...], sib_feat[...]], axis=0), jnp.concatenate(done_rows, axis=0))
+    qkv_sum.scatter(jnp.concatenate([qkv_part[:, :128], qkv_part[:, 128:]], axis=0))
+    final_rows.arrived()
+    gproj[:, CH : 2 * CH] = jnp.where(first_core, done_rows[0], gone_in[...])
+    gproj[:, 2 * CH :] = jnp.where(first_core, gone_in[...], done_rows[0])
+    gf[...] = ghid[...] + nt(gproj[...], wqkv[...])
+    rest_sum.spread()
     qkv_sum.along_z()
-    rest_sum.spread()
     qkv_sum.spread()
     rest_sum.swap()
     qkv_sum.swap()
     rest_sum.last()
-    qkv_sum.last()
 
     for group in (fg, dg, sg, rest_sum, qkv_sum):
         group.finish()
-    for message in (sib_f, down_fine, up_fine, sib_g, tri, parts, down_hid, up_hid, pairs):
+    for message in (sib_f, down_fine, up_fine, sib_g, tri, parts, pairs, final_rows):
         message.sent()
 
 
@@ -782,7 +803,7 @@
 
 
 def shards(features, qkv_weight, out_weight, conv_weight, grad_output):
-    messages = 2 * AG_MSGS + ST_MSGS + 2 * RS_MSGS + 9
+    messages = 2 * AG_MSGS + ST_MSGS + RS_MSGS + WIDE_MSGS + 10
     whole = pl.BlockSpec(memory_space=pltpu.VMEM)
     sums = pl.pallas_call(
         kernel,
@@ -800,13 +821,12 @@
             pltpu.VMEM((ROW, CH), BF16),
             pltpu.VMEM((ROW, CH), BF16),
             pltpu.VMEM((2, 2 * ROW, CO), BF16),
-            pltpu.VMEM((2, ROW, CH), BF16),
-            pltpu.VMEM((2, ROW, 4 * CO), BF16),
+            pltpu.VMEM((4, ROW, 4 * CO), BF16),
             pltpu.VMEM((CHUNKS, CHUNK, CH), BF16),
             pltpu.VMEM((CHUNKS, CHUNK, CH), BF16),
             pltpu.VMEM((CHUNKS, CHUNK, CH), BF16),
-            pltpu.VMEM((STACK, CH), BF16),
-            pltpu.VMEM((STACK, CH), BF16),
+            pltpu.VMEM((STACK, 128), BF16),
+            pltpu.VMEM((STACK, 128), BF16),
             pltpu.VMEM((CHUNKS * SLOT, 128), F32),
             pltpu.VMEM((CHUNKS * SLOT, 128), F32),
             pltpu.VMEM((PAIR, CHUNK), BF16),
@@ -823,8 +843,10 @@
             pltpu.VMEM((2, ROW, CH), F32),
             pltpu.VMEM((2, ROW, CH), F32),
             pltpu.VMEM((2, ROW, CH), F32),
-            pltpu.VMEM((ROW, 2 * CH), F32),
-            pltpu.VMEM((ROW, 2 * CH), F32),
+            pltpu.VMEM((2, ROW, CH), F32),
+            pltpu.VMEM((2, ROW, CH), F32),
+            pltpu.VMEM((ROW, CH), BF16),
+            pltpu.VMEM((ROW, CH), BF16),
             pltpu.VMEM((ROW, CH), F32),
             pltpu.VMEM((ROW, CH), BF16),
             pltpu.VMEM((ROW, 3 * CH), BF16),

time: 87.7 us -> 80.9 us (0.922)
  Pallas kernels: 86.9 us -> 80.1 us
    pallas_call x1, Pallas kernels: 84.2 us -> 77.4 us  [shards(): pl.pallas_call(kernel, out_shape=[jax.ShapeDtypeStruct((ROW, CH), F32), j...]
where the time goes in v4:
time: 80.9 us; the launch traced here: 80.7 us
  Pallas kernels  80.1 us (99%)
    pallas_call x1, Pallas kernels, shards(): pl.pallas_call(kernel, out_shape=[jax.ShapeDtypeStruct((ROW, CH), F32), j...  77.4 us
    pallas_call x1, Pallas kernels, shards(): pl.pallas_call(scale_out, out_shape=[jax.ShapeDtypeStruct((ROW, CH), F32)...  2.7 us

profile of v4, /device:TPU:1, one launch (start us, length us, event | category | flops | bytes accessed | tf_op | source)
XLA Modules:
  0.0 80.7 jit_solution(6623381066818768201)
XLA Ops:
  0.6 77.4 %shard_map.84 = (f32[128,256]{1,0:T(8,128)}, bf16[3584,128]{1,0:T(8,128)(2,1)}, bf16[1024,128]{1,0:T(8,128)(2,1)}) custom-call(bf16[128,256]{1,0:T(8,128)(2,1)} %bitcast.7, bf16[256,768]{1,0:T(8,128)(2,1)} %wqkv.1, bf16[256,256]{1,0:T(8,128)(2,1)} %wout.1, bf16[9,256,128]{2,1,0:T(8,128)(2,1)} %bitcast.5, bf16[2,256,128]{2,1,0:T(8,128)(2,1)} %bitcast.6), custom_call_target="tpu_custom_call" | custom-call | tf_op jit(solution)/shard_map/pallas_call | solution.py:808
  78.0 2.7 %shard_map.85 = (f32[128,256]{1,0:T(8,128)}, f32[256,768]{1,0:T(8,128)}, f32[256,256]{1,0:T(8,128)}, f32[2304,128]{1,0:T(8,128)}) custom-call(f32[128,256]{1,0:T(8,128)} %get-tuple-element.11.gf_in, bf16[3584,128]{1,0:T(8,128)(2,1)} %get-tuple-element.12.rest, bf16[1024,128]{1,0:T(8,128)(2,1)} %get-tuple-element.13.qkv), custom_call_target="tpu_custom_call" | custom-call | tf_op jit(solution)/shard_map/pallas_call | solution.py:871

commit v5 on v4

--- a/solution.py
+++ b/solution.py
@@ -24,7 +24,7 @@
 SLOT = RING * STACK
 REST_ROWS = 3584
 QKV_ROWS = 1024
-PLANE = [(k % 4, k // 4) for k in range(1, 16)]
+PLANE = sorted([(k % 4, k // 4) for k in range(1, 16)], key=lambda step: -sum(min(d, 4 - d) for d in step))
 AG_MSGS = 41
 ST_MSGS = 31
 RS_MSGS = 35
@@ -423,6 +423,9 @@
     def pack(*cells):
         return jnp.concatenate(cells, axis=1).astype(BF16)
 
+    def side(r):
+        return slice(r * 4 * CO, (r + 1) * 4 * CO)
+
     def taps(lines, a):
         w0, w1, w2 = wconv[3 * a], wconv[3 * a + 1], wconv[3 * a + 2]
         main = nt(lines, jnp.concatenate([w1, w0], axis=1)) + nt(lines, jnp.concatenate([w2, w1], axis=1))
@@ -440,7 +443,7 @@
     own_lines = []
     for r in (0, 1):
         even_cells, odd_cells = split(go[r])
-        sides[1 + r] = pack(even_cells, odd_cells, moved(even_cells, 1), moved(odd_cells, -1))
+        sides[:, side(1 + r)] = pack(even_cells, odd_cells, moved(even_cells, 1), moved(odd_cells, -1))
         own_lines.append(pack(even_cells, odd_cells))
     middle = taps(jnp.concatenate(own_lines, axis=0), 1)
     local = [
@@ -470,7 +473,7 @@
     outer = []
     for r, inside in ((0, s > 0), (1, s < 63)):
         even_cells, odd_cells = (jnp.where(inside, cells, 0.0) for cells in split(fine[r]))
-        sides[3 * r] = pack(even_cells, odd_cells, moved(even_cells, 1), moved(odd_cells, -1))
+        sides[:, side(3 * r)] = pack(even_cells, odd_cells, moved(even_cells, 1), moved(odd_cells, -1))
         outer.append(pack(even_cells, odd_cells))
     top, bottom = outer
     main, plus, minus = (m + f + l for m, f, l in zip(local, taps(bottom, 0), taps(top, 2), strict=True))
@@ -692,7 +695,8 @@
 
     def conv_rows():
         mid = hid[...]
-        met = [tn(mid, sides[r]) for r in range(4)]
+        every = tn(mid, sides[...])
+        met = [every[:, side(r)] for r in range(4)]
         part = rest_sum.part
         for a, whole in enumerate((met[2] + met[3], met[1] + met[2], met[0] + met[1])):
             even_c, odd_c, even1, odd1 = (whole[:, k * CO : (k + 1) * CO] for k in range(4))
@@ -737,8 +741,6 @@
             j = 2 * jj + p
             if final and p == 0:
                 dg.last(1)
-            if final and p == 1:
-                rest_sum.along_z()
             if not final:
                 steps(jj, p, {0: first_sums, 2: rest_sum.scatter, 3: before_four})
             before = jnp.maximum(j - 1, 0)
@@ -767,6 +769,7 @@
         pair_out[1 - half] = jnp.where(first_core, gv, gk)
         own_part.append(jnp.where(first_core, gk, gv))
     pairs.start()
+    rest_sum.along_z()
     pairs.arrived()
     done_rows = [(own_part[half] + pair_in[half]).astype(BF16) for half in (0, 1)]
     gone_out[...] = done_rows[1]
@@ -821,7 +824,7 @@
             pltpu.VMEM((ROW, CH), BF16),
             pltpu.VMEM((ROW, CH), BF16),
             pltpu.VMEM((2, 2 * ROW, CO), BF16),
-            pltpu.VMEM((4, ROW, 4 * CO), BF16),
+            pltpu.VMEM((ROW, 16 * CO), BF16),
             pltpu.VMEM((CHUNKS, CHUNK, CH), BF16),
             pltpu.VMEM((CHUNKS, CHUNK, CH), BF16),
             pltpu.VMEM((CHUNKS, CHUNK, CH), BF16),

time: 80.9 us -> 79.4 us (0.981)
  Pallas kernels: 80.1 us -> 78.6 us
    pallas_call x1, Pallas kernels: 77.4 us -> 75.9 us  [shards(): pl.pallas_call(kernel, out_shape=[jax.ShapeDtypeStruct((ROW, CH), F32), j...]
where the time goes in v5:
time: 79.4 us; the launch traced here: 79.2 us
  Pallas kernels  78.6 us (99%)
    pallas_call x1, Pallas kernels, shards(): pl.pallas_call(kernel, out_shape=[jax.ShapeDtypeStruct((ROW, CH), F32), j...  75.9 us
    pallas_call x1, Pallas kernels, shards(): pl.pallas_call(scale_out, out_shape=[jax.ShapeDtypeStruct((ROW, CH), F32)...  2.7 us

profile of v5, /device:TPU:1, one launch (start us, length us, event | category | flops | bytes accessed | tf_op | source)
XLA Modules:
  0.0 79.2 jit_solution(13658544181982882533)
XLA Ops:
  0.6 75.9 %shard_map.84 = (f32[128,256]{1,0:T(8,128)}, bf16[3584,128]{1,0:T(8,128)(2,1)}, bf16[1024,128]{1,0:T(8,128)(2,1)}) custom-call(bf16[128,256]{1,0:T(8,128)(2,1)} %bitcast.7, bf16[256,768]{1,0:T(8,128)(2,1)} %wqkv.1, bf16[256,256]{1,0:T(8,128)(2,1)} %wout.1, bf16[9,256,128]{2,1,0:T(8,128)(2,1)} %bitcast.5, bf16[2,256,128]{2,1,0:T(8,128)(2,1)} %bitcast.6), custom_call_target="tpu_custom_call" | custom-call | tf_op jit(solution)/shard_map/pallas_call | solution.py:811
  76.5 2.7 %shard_map.85 = (f32[128,256]{1,0:T(8,128)}, f32[256,768]{1,0:T(8,128)}, f32[256,256]{1,0:T(8,128)}, f32[2304,128]{1,0:T(8,128)}) custom-call(f32[128,256]{1,0:T(8,128)} %get-tuple-element.11.gf_in, bf16[3584,128]{1,0:T(8,128)(2,1)} %get-tuple-element.12.rest, bf16[1024,128]{1,0:T(8,128)(2,1)} %get-tuple-element.13.qkv), custom_call_target="tpu_custom_call" | custom-call | tf_op jit(solution)/shard_map/pallas_call | solution.py:874

commit v6 on v5

--- a/solution.py
+++ b/solution.py
@@ -417,7 +417,7 @@
         pl.semaphore_signal(barrier, inc=1, device_id=peer, device_id_type=MESH)
 
     def split(rows):
-        wide[...] = rows.astype(F32)
+        wide[: 2 * ROW] = rows.astype(F32)
         return wide[pl.ds(0, ROW, stride=2)], wide[pl.ds(1, ROW, stride=2)]
 
     def pack(*cells):
@@ -854,7 +854,7 @@
             pltpu.VMEM((ROW, CH), BF16),
             pltpu.VMEM((ROW, 3 * CH), BF16),
             pltpu.VMEM((ROW, CH), BF16),
-            pltpu.VMEM((2 * ROW, CO), F32),
+            pltpu.VMEM((2 * ROW + 8, CO), F32),
             *total_scratch(REST_ROWS),
             *total_scratch(QKV_ROWS),
             pltpu.SemaphoreType.DMA((messages,)),

time: 79.4 us -> 79.4 us (level)
  no operation moved by 1% of the time
where the time goes in v6:
time: 79.4 us; the launch traced here: 79.2 us
  Pallas kernels  78.6 us (99%)
    pallas_call x1, Pallas kernels, shards(): pl.pallas_call(kernel, out_shape=[jax.ShapeDtypeStruct((ROW, CH), F32), j...  75.9 us
    pallas_call x1, Pallas kernels, shards(): pl.pallas_call(scale_out, out_shape=[jax.ShapeDtypeStruct((ROW, CH), F32)...  2.7 us

profile of v6, /device:TPU:1, one launch (start us, length us, event | category | flops | bytes accessed | tf_op | source)
XLA Modules:
  0.0 79.2 jit_solution(17525615938758194581)
XLA Ops:
  0.6 75.9 %shard_map.84 = (f32[128,256]{1,0:T(8,128)}, bf16[3584,128]{1,0:T(8,128)(2,1)}, bf16[1024,128]{1,0:T(8,128)(2,1)}) custom-call(bf16[128,256]{1,0:T(8,128)(2,1)} %bitcast.7, bf16[256,768]{1,0:T(8,128)(2,1)} %wqkv.1, bf16[256,256]{1,0:T(8,128)(2,1)} %wout.1, bf16[9,256,128]{2,1,0:T(8,128)(2,1)} %bitcast.5, bf16[2,256,128]{2,1,0:T(8,128)(2,1)} %bitcast.6), custom_call_target="tpu_custom_call" | custom-call | tf_op jit(solution)/shard_map/pallas_call | solution.py:811
  76.5 2.7 %shard_map.85 = (f32[128,256]{1,0:T(8,128)}, f32[256,768]{1,0:T(8,128)}, f32[256,256]{1,0:T(8,128)}, f32[2304,128]{1,0:T(8,128)}) custom-call(f32[128,256]{1,0:T(8,128)} %get-tuple-element.11.gf_in, bf16[3584,128]{1,0:T(8,128)(2,1)} %get-tuple-element.12.rest, bf16[1024,128]{1,0:T(8,128)(2,1)} %get-tuple-element.13.qkv), custom_call_target="tpu_custom_call" | custom-call | tf_op jit(solution)/shard_map/pallas_call | solution.py:874
